TPU v7x, 512 devices: a whole 4x4x16 slice. The times are simulated.
512 devices in a mesh: heads: 8 (over x, y_lo), seq: 64 (over z, y_hi, core).
Axes of the slice: x: 4, y: 4 (y_hi: 2, y_lo: 2; y = y_hi * 2 + y_lo), z: 16, core: 2. Of those that a mesh axis runs over, the one named last changes fastest.
Arguments:
- query_nope: bfloat16 [1, 4, 128, 128], P(None, None, 'heads'), may hold values from -6 to 6
- query_rope: bfloat16 [1, 4, 128, 64], P(None, None, 'heads'), may hold values from -8 to 8
- latent_cache: bfloat16 [1, 32768, 512], P(None, 'seq'), may hold values from -6 to 6
- rope_keys: bfloat16 [1, 64, 32768], P(None, None, 'seq'), may hold values from -8 to 8
- lengths: int32 [1], replicated, may hold values from 2 to 32765, as said below
- key_quant: bfloat16 [128, 512, 128], P('heads', 'seq'), may hold values from -127 to 127, as said below
- key_scale: float32 [128, 4], P('heads'), may hold values from 0.0006 to 0.0024
- value_quant: bfloat16 [128, 512, 128], P('heads', 'seq'), may hold values from -127 to 127, as said below
- value_scale: float32 [128, 4], P('heads'), may hold values from 0.0003 to 0.0012
- out_weight: bfloat16 [16384, 7168], P('heads', 'seq'), may hold values from -0.375 to 0.375
Outputs:
- attn_out: bfloat16 [1, 4, 7168], P(None, None, 'seq')
Inputs may be any that keep to these rules, and one draw needn't show every extreme that they name: `key_quant`: whole numbers. `value_quant`: whole numbers. `lengths`: one sequence has the largest allowed length, so that its last draft token sees all 32768 positions.
All inputs are finite; a program needn't handle non-finite values.
Results may differ from a plain program's by a relative error of at most 0.019.
Values may be sent and summed in bfloat16 or wider, within the bound.
No kernel may reach another device: no remote copies, remote signals or barrier semaphores. Data moves between devices by JAX's collectives and lax.ppermute only.
A program may use at most 64 MiB of HBM per device.

v0:
```python
import jax
import jax.numpy as jnp
from jax import lax
from jax.sharding import PartitionSpec as P

QB = 128


neg_large = -1e30


def laid_out(parts, dim):
    lengths = list(parts.shape[1:])
    lengths[dim] *= parts.shape[0]
    return jnp.moveaxis(parts, 0, dim).reshape(lengths)


def from_everyone(x, axis):
    length = lax.axis_size(axis)
    return lax.all_to_all(jnp.broadcast_to(x[None], (length, *x.shape)), axis, 0, 0, tiled=True)


def gather_directly(x, axis, dim):
    return laid_out(from_everyone(x, axis), dim)


def gathered_once(x, axis):
    leaves = jax.tree.leaves(x)
    sequence = sorted(range(len(leaves)), key=lambda k: -leaves[k].size)
    width = (1, *leaves[sequence[0]].shape)[-1]
    lines = [
        jnp.pad(leaves[k].reshape(-1), (0, -leaves[k].size % width)).reshape(-1, width)
        for k in sequence
    ]
    both, at, found = (from_everyone(jnp.concatenate(lines), axis), 0, {})
    for k, line in zip(sequence, lines):
        piece = both[:, at : at + len(line)].reshape(len(both), -1)
        found[k] = piece[:, : leaves[k].size].reshape(-1, *leaves[k].shape)
        at += len(line)
    numbers = iter(range(len(leaves)))
    return jax.tree.map(lambda _: found[next(numbers)], x)


def combined_pairwise(pieces, combine):
    while len(jax.tree.leaves(pieces)[0]) > 1:
        pieces = jax.vmap(combine)(
            *(jax.tree.map(lambda part: part[side::2], pieces) for side in (0, 1))
        )
    return jax.tree.map(lambda part: part[0], pieces)


def joined_all(x, axis, combine):
    pieces = gathered_once(x, axis)
    return combined_pairwise(pieces, combine)


def split_up(x, dim, length):
    before, after = (x.shape[:dim], x.shape[dim + 1 :])
    return jnp.moveaxis(x.reshape(*before, length, -1, *after), dim, 0)


def sum_at_owner(x, axis, dim):
    length = lax.axis_size(axis)
    parts = lax.all_to_all(split_up(x, dim, length), axis, 0, 0, tiled=True)
    return jnp.sum(parts, axis=0)


def over_copies(x, axis):
    return from_everyone(x, axis).sum(axis=0)


def expand_scales(block_scale, offset, count):
    row_ids = (offset + jnp.arange(count, dtype=jnp.int32)) // QB
    onehot = (
        row_ids[:, None] == jnp.arange(block_scale.shape[1], dtype=jnp.int32)[None, :]
    ).astype(block_scale.dtype)
    return jnp.sum(block_scale[:, None, :] * onehot[None, :, :], axis=2)


def dequantize(quantized, block_scale, offset):
    factors = expand_scales(block_scale, offset, quantized.shape[1])
    return (quantized.astype(jnp.float32) * factors[:, :, None]).astype(jnp.bfloat16)


def combine_stats(earlier, later):
    max_a, sum_a = earlier
    max_b, sum_b = later
    joint = jnp.maximum(max_a, max_b)
    return (joint, sum_a * jnp.exp(max_a - joint) + sum_b * jnp.exp(max_b - joint))


def per_device(
    query_nope,
    query_rope,
    latent_cache,
    rope_keys,
    lengths,
    key_quant,
    key_scale,
    value_quant,
    value_scale,
    out_weight,
):
    seq_index = lax.axis_index("seq")
    latent_cols = key_quant.shape[1]
    offset = seq_index * latent_cols
    factor = (query_nope.shape[-1] + query_rope.shape[-1]) ** (-0.5)
    key_weight = dequantize(key_quant, key_scale, offset)
    piece_lat = jnp.einsum(
        "btkn,kcn->btkc", query_nope, key_weight, preferred_element_type=jnp.float32
    ).astype(jnp.bfloat16)
    query_latent = gather_directly(piece_lat, "seq", 3)
    positions = latent_cache.shape[1]
    scores = jnp.einsum(
        "btkc,bsc->btks", query_latent, latent_cache, preferred_element_type=jnp.float32
    )
    scores = (
        scores
        + jnp.einsum("btkr,brs->btks", query_rope, rope_keys, preferred_element_type=jnp.float32)
    ) * factor
    position = seq_index * positions + jnp.arange(positions, dtype=jnp.int32)
    horizon = lengths[:, None] + jnp.arange(query_nope.shape[1], dtype=jnp.int32)[None, :]
    visible = (position[None, None, :] < horizon[:, :, None])[:, :, None, :]
    block_max = jnp.max(jnp.where(visible, scores, neg_large), axis=3)
    probs = jnp.where(visible, jnp.exp(scores - block_max[..., None]), 0.0)
    block_sum = jnp.sum(probs, axis=3)
    probs_bf = probs.astype(jnp.bfloat16)
    block_out = jnp.einsum(
        "btks,bsc->btkc", probs_bf, latent_cache, preferred_element_type=jnp.float32
    )
    top, totals = joined_all((block_max, block_sum), "seq", combine_stats)
    shrink = jnp.exp(block_max - top)
    merged_slice = sum_at_owner(block_out * shrink[..., None], "seq", 3)
    latent_slice = (merged_slice / totals[..., None]).astype(jnp.bfloat16)
    value_weight = dequantize(value_quant, value_scale, offset)
    partial_heads = jnp.einsum(
        "btkc,kcv->btkv", latent_slice, value_weight, preferred_element_type=jnp.float32
    )
    flat_terms = partial_heads.reshape(-1)
    share_sum = sum_at_owner(flat_terms, "seq", 0).astype(jnp.bfloat16)
    head_output = gather_directly(share_sum, "seq", 0).reshape(partial_heads.shape)
    batch, drafts, heads_here, value_width = head_output.shape
    projected = jnp.dot(
        head_output.reshape(batch * drafts, heads_here * value_width),
        out_weight,
        preferred_element_type=jnp.float32,
    )
    summed = over_copies(projected, "heads")
    return summed.astype(jnp.bfloat16).reshape(batch, drafts, out_weight.shape[1])


def solution(mesh):
    in_specs = (
        P(None, None, "heads", None),
        P(None, None, "heads", None),
        P(None, "seq", None),
        P(None, None, "seq"),
        P(),
        P("heads", "seq", None),
        P("heads", None),
        P("heads", "seq", None),
        P("heads", None),
        P("heads", "seq"),
    )
    out_specs = P(None, None, "seq")
    return jax.shard_map(
        per_device, mesh=mesh, in_specs=in_specs, out_specs=out_specs, check_vma=False
    )
```

profile of v0, /device:TPU:1, one launch (start us, length us, event | category | flops | bytes accessed | tf_op | source)
XLA Modules:
  0.0 138.7 jit_solution(4470355562503307247)
XLA Ops:
  0.1 0.7 copy-done.4
  0.9 1.0 fusion.1
  2.1 1.1 reshape.207
  3.1 19.9 %all-to-all-start = ((bf16[64,2,256]{2,1,0:T(2,128)(2,1)}), bf16[64,2,256]{2,1,0:T(2,128)(2,1)S(1)}, u32[]{:S(2)}, u32[]{:S(2)}) async-start(bf16[64,2,256]{2,1,0:T(2,128)(2,1)} %reshape.207), calls=%async_computation | async-start | bytes 131072 | tf_op jit(solution)/shard_map/all_to_all | solution.py:20
  23.9 15.0 %all-to-all-done = bf16[64,2,256]{2,1,0:T(2,128)(2,1)S(1)} async-done(((bf16[64,2,256]{2,1,0:T(2,128)(2,1)}), bf16[64,2,256]{2,1,0:T(2,128)(2,1)S(1)}, u32[]{:S(2)}, u32[]{:S(2)}) %all-to-all-start) | async-done | bytes 65568 | tf_op jit(solution)/shard_map/all_to_all | solution.py:20
  39.0 0.4 reshape.208
  39.4 0.5 select_reduce_fusion
  40.3 18.4 %all_to_all.35 = f32[64,1,128]{2,1,0:T(1,128)S(1)} all-to-all(f32[64,1,128]{2,1,0:T(1,128)S(1)} %reshape.209), channel_id=1, replica_groups=mesh['heads'=8,'seq'=64] {'seq'}, dimensions={0} | all-to-all | bytes 65536 | tf_op jit(solution)/shard_map/all_to_all | solution.py:20
  58.7 0.5 broadcast.121
  59.2 0.7 reduce.11
  60.2 0.3 slice.83
  60.6 0.3 slice.84
  61.0 0.3 slice.96
  61.3 0.3 slice.97
  61.7 0.2 slice.85
  61.9 0.2 slice.86
  62.1 0.2 slice.98
  62.3 0.2 slice.99
  64.2 0.3 convolution_multiply_fusion
  64.4 0.3 copy.114
  64.9 1.0 reshape.211
  65.9 4.7 %all-to-all-start.2 = ((f32[64,1,512]{2,1,0:T(1,128)}), f32[64,1,512]{2,1,0:T(1,128)S(1)}, u32[]{:S(2)}, u32[]{:S(2)}) async-start(f32[64,1,512]{2,1,0:T(1,128)} %reshape.211), calls=%async_computation.2 | async-start | bytes 262144 | tf_op jit(solution)/shard_map/all_to_all | solution.py:64
  70.7 18.6 %all-to-all-done.2 = f32[64,1,512]{2,1,0:T(1,128)S(1)} async-done(((f32[64,1,512]{2,1,0:T(1,128)}), f32[64,1,512]{2,1,0:T(1,128)S(1)}, u32[]{:S(2)}, u32[]{:S(2)}) %all-to-all-start.2) | async-done | bytes 131104 | tf_op jit(solution)/shard_map/all_to_all | solution.py:64
  89.3 1.0 reduce.12
  90.3 0.4 reshape.212
  90.9 0.5 copy-done.6
  91.4 0.2 convolution_bitcast_fusion
  91.6 18.4 %all_to_all.36 = f32[64,1,128]{2,1,0:T(1,128)S(1)} all-to-all(f32[64,1,128]{2,1,0:T(1,128)S(1)} %bitcast.67), channel_id=1, replica_groups=mesh['heads'=8,'seq'=64] {'seq'}, dimensions={0} | all-to-all | bytes 65536 | tf_op jit(solution)/shard_map/all_to_all | solution.py:64
  110.2 18.7 %all_to_all.37 = bf16[64,1,128]{2,1,0:T(2,128)(2,1)S(1)} all-to-all(bf16[64,1,128]{2,1,0:T(2,128)(2,1)S(1)} %broadcast_in_dim.34), channel_id=1, replica_groups=mesh['heads'=8,'seq'=64] {'seq'}, dimensions={0} | all-to-all | bytes 32768 | tf_op jit(solution)/shard_map/all_to_all | solution.py:20
  128.9 0.2 fusion.23
  129.2 9.0 %all_to_all.38 = f32[8,4,112]{2,1,0:T(4,128)S(1)} all-to-all(f32[8,4,112]{2,1,0:T(4,128)S(1)} %broadcast_in_dim.35), channel_id=1, replica_groups=mesh['heads'=8,'seq'=64] {'heads'}, dimensions={0} | all-to-all | bytes 28672 | tf_op jit(solution)/shard_map/all_to_all | solution.py:20
  138.1 0.6 reduce_sum.59
  (62 shorter events, 3.5 us)
Async XLA Ops:
  0.0 39.4 %copy-start = (bf16[1,512,512]{2,1,0:T(8,128)(2,1)S(1)}, bf16[1,512,512]{2,1,0:T(8,128)(2,1)}, u32[]{:S(2)}) copy-start(bf16[1,512,512]{2,1,0:T(8,128)(2,1)} %param.12) | copy-start | bytes 1572868
  0.0 0.7 copy-start.4
  0.0 0.8 copy-start.5
  0.0 0.9 copy-start.7
  3.1 20.7 %copy-start.2 = (bf16[1,64,512]{2,1,0:T(8,128)(2,1)S(1)}, bf16[1,64,512]{2,1,0:T(8,128)(2,1)}, u32[]{:S(2)}) copy-start(bf16[1,64,512]{2,1,0:T(8,128)(2,1)} %param.13) | copy-start | bytes 196612
  3.1 20.7 %copy-start.3 = (bf16[1,4,16,64]{3,2,1,0:T(8,128)(2,1)S(1)}, bf16[1,4,16,64]{3,2,1,0:T(8,128)(2,1)}, u32[]{:S(2)}) copy-start(bf16[1,4,16,64]{3,2,1,0:T(8,128)(2,1)} %param.11) | copy-start | bytes 24580
  3.1 35.9 %all-to-all-start = ((bf16[64,2,256]{2,1,0:T(2,128)(2,1)}), bf16[64,2,256]{2,1,0:T(2,128)(2,1)S(1)}, u32[]{:S(2)}, u32[]{:S(2)}) async-start(bf16[64,2,256]{2,1,0:T(2,128)(2,1)} %reshape.207), calls=%async_computation | async-start | bytes 131072 | tf_op jit(solution)/shard_map/all_to_all | solution.py:20
  65.9 23.4 %all-to-all-start.2 = ((f32[64,1,512]{2,1,0:T(1,128)}), f32[64,1,512]{2,1,0:T(1,128)S(1)}, u32[]{:S(2)}, u32[]{:S(2)}) async-start(f32[64,1,512]{2,1,0:T(1,128)} %reshape.211), calls=%async_computation.2 | async-start | bytes 262144 | tf_op jit(solution)/shard_map/all_to_all | solution.py:64
  90.6 0.8 copy-start.6
  90.7 38.2 %copy-start.1 = (bf16[2048,112]{0,1:T(8,128)(2,1)S(1)}, bf16[2048,112]{0,1:T(8,128)(2,1)}, u32[]{:S(2)}) copy-start(bf16[2048,112]{0,1:T(8,128)(2,1)} %param.19) | copy-start | bytes 1376260
where the time goes:
time: 139 us
  blocking collectives  64.5 us (46%)
  waiting for transfers between devices  33.7 us (24%)
  starting transfers between devices  24.6 us (18%)
  local copies, waits for them, and re-layouts  9.43 us (7%)
  other arithmetic  3.21 us (2%)
  matrix products  2.27 us (2%)
    all_to_all x3, blocking collectives, from_everyone(): lax.all_to_all(jnp.broadcast_to(x[None], (length, *x.shape)), axis, 0, 0,...  46.1 us
    all_to_all x1, starting transfers between devices, from_everyone(): lax.all_to_all(jnp.broadcast_to(x[None], (length, *x.shape)), axis, 0, 0,...  19.9 us
    all_to_all x1, waiting for transfers between devices, sum_at_owner(): parts = lax.all_to_all(split_up(x, dim, length), axis, 0, 0, tiled=True)  18.6 us
    all_to_all x1, blocking collectives, sum_at_owner(): parts = lax.all_to_all(split_up(x, dim, length), axis, 0, 0, tiled=True)  18.4 us
    all_to_all x1, waiting for transfers between devices, from_everyone(): lax.all_to_all(jnp.broadcast_to(x[None], (length, *x.shape)), axis, 0, 0,...  15 us
    unnamed x26, local copies, waits for them, and re-layouts  4.74 us
    all_to_all x1, starting transfers between devices, sum_at_owner(): parts = lax.all_to_all(split_up(x, dim, length), axis, 0, 0, tiled=True)  4.67 us
    slice x20, local copies, waits for them, and re-layouts, combined_pairwise(): part[side::2]  3.4 us
  transfers between devices with their start and end apart: 2, of which 2 were waited for; matrix products, arithmetic and copies ran while one was open for 0% of the time, Pallas kernels for 0%

commit v1 on v0

v1 whole, which is shorter than its diff:
```python
import jax
import jax.numpy as jnp
from jax import lax
from jax.experimental import pallas as pl
from jax.experimental.pallas import tpu as pltpu
from jax.sharding import Mesh, PartitionSpec as P

QB = 128
RUN = 16
LANES = 128
NEG = -1e30
F32 = jnp.float32
BF16 = jnp.bfloat16
SMEM = pl.BlockSpec(memory_space=pltpu.SMEM)
HBM = pl.BlockSpec(memory_space=pltpu.HBM)
VMEM = pl.BlockSpec(memory_space=pltpu.VMEM)


def iota(shape, dim):
    return lax.broadcasted_iota(jnp.int32, shape, dim)


def dot(a, b, dims=((1,), (0,))):
    return lax.dot_general(a, b, (dims, ((), ())), preferred_element_type=F32)


def head_major(drafts, heads, copies):
    rows = drafts * heads
    col = iota((rows, copies * rows), 1) % rows
    source = (col % drafts) * heads + col // drafts
    return (iota((rows, copies * rows), 0) == source).astype(BF16)


def query_kernel(block_ref, scale_hbm, query_hbm, quant_hbm, out_ref, scale_ref, query_ref, quant_ref, sems):
    copies = [
        pltpu.make_async_copy(source, target, sems.at[k])
        for k, (source, target) in enumerate(
            ((quant_hbm, quant_ref), (query_hbm, query_ref), (scale_hbm, scale_ref))
        )
    ]
    for copy in copies:
        copy.start()
    for copy in copies:
        copy.wait()
    heads, cols, width = quant_ref.shape
    rows = query_ref.shape[0]
    block = block_ref[0]
    weight = jnp.concatenate(
        [(quant_ref[h].astype(F32) * scale_ref[block, h]).astype(BF16) for h in range(heads)], axis=0
    )
    both = dot(weight, query_ref[...], ((1,), (1,)))
    own = iota(both.shape, 0) // cols == iota(both.shape, 1) % heads
    piece = jnp.sum(jnp.where(own, both, 0.0).reshape(heads, cols, rows), axis=0)
    moved = dot(piece.astype(BF16), head_major(rows // heads, heads, 2))
    low = iota((cols // 2, 2 * rows), 1) < rows
    folded = jnp.where(low, moved[: cols // 2], moved[cols // 2 :]).astype(BF16)
    out_ref[...] = jnp.broadcast_to(folded[None], out_ref.shape)


def value_kernel(place_ref, scale_ref, quant_ref, out_ref):
    block, run = place_ref[0], place_ref[1]
    for h in range(quant_ref.shape[0]):
        out_ref[h ^ run] = (quant_ref[h].astype(F32) * scale_ref[block, h]).astype(BF16)


def ready_kernel(query_ref, key_ref, cache_ref, rope_ref, moved_ref):
    rows = query_ref.shape[0]
    latent = cache_ref.shape[1]
    drafts = rows // RUN
    query = dot(head_major(drafts, RUN, 1), query_ref[...], ((0,), (0,))).astype(BF16)
    rope_ref[...] = dot(query, key_ref[...])
    new = iota((latent, latent), 1)
    half, at = new // (latent // 2), new % (latent // 2)
    source = (at // 4) * 8 + half * 4 + at % 4
    order = (iota((latent, latent), 0) == source).astype(BF16)
    moved_ref[...] = dot(cache_ref[...], order).astype(BF16)


def split3(x):
    high = x.astype(BF16).astype(F32)
    middle = (x - high).astype(BF16).astype(F32)
    return high, middle, x - high - middle


def attend_kernel(factor, length_ref, start_ref, queries_ref, rope_ref, moved_ref, cache_ref, out_ref):
    rows, positions = rope_ref.shape
    senders, fold, _ = queries_ref.shape
    drafts = rows // RUN
    queries = queries_ref[...].reshape(senders * fold, 2 * rows)
    queries = jnp.concatenate([queries[:, :rows], queries[:, rows:]], axis=0)
    scores = (dot(queries, moved_ref[...], ((0,), (1,))) + rope_ref[...]) * factor
    position = start_ref[0] + iota(scores.shape, 1)
    visible = position < length_ref[0] + iota(scores.shape, 0) % drafts
    top = jnp.max(jnp.where(visible, scores, NEG), axis=1, keepdims=True)
    probs = jnp.where(visible, jnp.exp(scores - top), 0.0)
    total = jnp.sum(probs, axis=1, keepdims=True)
    out = dot(probs.astype(BF16), cache_ref[...])
    lane = iota((rows, LANES), 1)
    stats = jnp.zeros(lane.shape, F32)
    for k, part in enumerate((*split3(top), *split3(total))):
        stats = jnp.where(lane % 8 == k, part, stats)
    low = iota((2, LANES), 1) < 8
    for h in range(RUN):
        at = h * drafts
        both = jnp.where(low, stats[at : at + 2], stats[at + 2 : at + 4]).astype(BF16)
        for q in range(out_ref.shape[0] // RUN):
            columns = slice(q * LANES, (q + 1) * LANES)
            for k in range(drafts // 2):
                out_ref[q * RUN + h, k] = out[at + 2 * k : at + 2 * k + 2, columns].astype(BF16)
            out_ref[q * RUN + h, drafts // 2] = both


def head_kernel(run_ref, parts_ref, value_ref, out_ref):
    run = run_ref[0]
    pairs = parts_ref.shape[1] - 1
    stats = parts_ref[:, pairs].astype(F32)
    latents = []
    for k in range(pairs):
        tops, sums = (
            sum(stats[:, :, 8 * k + at + i : 8 * k + at + i + 1] for i in range(3)) for at in (0, 3)
        )
        shrink = jnp.exp(tops - jnp.max(tops, axis=0, keepdims=True))
        total = jnp.sum(sums * shrink, axis=0)
        merged = jnp.sum(parts_ref[:, k].astype(F32) * shrink, axis=0)
        latents.append(merged / total)
    latent = jnp.concatenate(latents, axis=0).astype(BF16)
    weight = jnp.concatenate([value_ref[j ^ run] for j in range(RUN)], axis=0)
    out_ref[...] = jnp.broadcast_to(dot(latent, weight).astype(BF16)[None], out_ref.shape)


def project_kernel(parts_ref, weight_ref, out_ref):
    devices = parts_ref.shape[0]
    heads = sum(parts_ref[q * RUN : (q + 1) * RUN].astype(F32) for q in range(devices // RUN)).astype(BF16)
    flat = jnp.concatenate([heads[h] for h in range(RUN)], axis=1)
    term = dot(flat, weight_ref[...], ((1,), (1,)))
    out_ref[...] = jnp.broadcast_to(term[None], out_ref.shape)


def call(kernel, shapes, specs, dtypes=BF16, scratch=()):
    if isinstance(dtypes, tuple):
        out_shape = [jax.ShapeDtypeStruct(s, d) for s, d in zip(shapes, dtypes)]
        out_specs = [VMEM] * len(shapes)
    else:
        out_shape, out_specs = jax.ShapeDtypeStruct(shapes, dtypes), VMEM
    return pl.pallas_call(
        kernel,
        out_shape=out_shape,
        in_specs=specs,
        out_specs=out_specs,
        scratch_shapes=scratch,
        compiler_params=pltpu.CompilerParams(vmem_limit_bytes=32 * 1024 * 1024),
    )


def exchange(blocks):
    blocks = blocks[None]
    for step in (8, 4, 2, 1):
        kept, sent = blocks[:, :step], blocks[:, step:]
        came = lax.ppermute(sent, "run", [(i, i ^ step) for i in range(RUN)])
        blocks = jnp.stack([kept, came], axis=0 if step == 8 else 1).reshape(-1, step, *blocks.shape[2:])
    return blocks[:, 0]


def per_device(
    query_nope,
    query_rope,
    latent_cache,
    rope_keys,
    lengths,
    key_quant,
    key_scale,
    value_quant,
    value_scale,
    out_weight,
):
    seq = ("quarter", "run")
    groups, quarters = lax.axis_size("heads"), lax.axis_size("quarter")
    devices = quarters * RUN
    _, drafts, heads, width = query_nope.shape
    rows = drafts * heads
    rope_width = query_rope.shape[3]
    _, positions, latent = latent_cache.shape
    cols = key_quant.shape[1]
    mine = out_weight.shape[1]
    run = lax.axis_index("run").astype(jnp.int32)
    place = lax.axis_index("quarter").astype(jnp.int32) * RUN + run
    block = (place * cols) >> 7
    start = place * positions
    factor = (width + rope_width) ** (-0.5)

    pieces = call(
        query_kernel,
        (devices, cols // 2, 2 * rows),
        [SMEM, HBM, HBM, HBM],
        scratch=(
            pltpu.SMEM(key_scale.T.shape, F32),
            pltpu.VMEM((rows, width), BF16),
            pltpu.VMEM(key_quant.shape, BF16),
            pltpu.SemaphoreType.DMA((3,)),
        ),
    )(block[None], key_scale.T, query_nope.reshape(rows, width), key_quant)
    queries = lax.all_to_all(pieces, seq, 0, 0, tiled=True)

    values = exchange(
        call(value_kernel, value_quant.shape, [SMEM, SMEM, VMEM])(
            jnp.stack([block, run]), value_scale.T, value_quant
        )
    )

    rope, moved = call(
        ready_kernel, ((rows, positions), (positions, latent)), [VMEM] * 3, (F32, BF16)
    )(query_rope.reshape(rows, rope_width), rope_keys[0], latent_cache[0])
    parts = call(
        lambda *refs: attend_kernel(factor, *refs),
        (devices, drafts // 2 + 1, 2, LANES),
        [SMEM, SMEM] + [VMEM] * 4,
    )(lengths, start[None], queries, rope, moved, latent_cache[0])
    parts = lax.all_to_all(parts, seq, 0, 0, tiled=True)

    terms = call(head_kernel, (devices, drafts, value_quant.shape[2]), [SMEM, VMEM, VMEM])(
        run[None], parts, values
    )
    terms = lax.all_to_all(terms, seq, 0, 0, tiled=True)
    sums = call(project_kernel, (groups, drafts, mine), [VMEM, VMEM], F32)(terms, out_weight.T)
    sums = lax.all_to_all(sums, "heads", 0, 0, tiled=True)
    return jnp.sum(sums, axis=0).astype(BF16)[None]


def solution(mesh):
    sizes = (mesh.shape["heads"], mesh.shape["seq"] // RUN, RUN)
    finer = Mesh(mesh.devices.reshape(sizes), ("heads", "quarter", "run"))
    seq = ("quarter", "run")
    in_specs = (
        P(None, None, "heads", None),
        P(None, None, "heads", None),
        P(None, seq, None),
        P(None, None, seq),
        P(),
        P("heads", seq, None),
        P("heads", None),
        P("heads", seq, None),
        P("heads", None),
        P("heads", seq),
    )
    out_specs = P(None, None, seq)
    return jax.shard_map(
        per_device, mesh=finer, in_specs=in_specs, out_specs=out_specs, check_vma=False
    )
```

time: 139 us -> 105 us (0.76)
  blocking collectives: 64.5 us -> 28.7 us
  starting transfers between devices: 24.6 us -> 40 us
  waiting for transfers between devices: 33.7 us -> 25.7 us
  local copies, waits for them, and re-layouts: 9.43 us -> 3.69 us
  Pallas kernels: 0 us -> 4.87 us
  other arithmetic: 3.21 us -> 0.68 us
  matrix products: 2.27 us -> 0 us
    all_to_all x4 -> x2, blocking collectives: 64.5 us -> 28.7 us  [the longest x1 19.7 us: per_device(): terms = lax.all_to_all(terms, seq, 0, 0, tiled=True)]
    ppermute x0 -> x4, starting transfers between devices: none -> 16.5 us  [exchange(): came = lax.ppermute(sent, 'run', [(i, i ^ step) for i in range(RUN)])]
    all_to_all x2, waiting for transfers between devices: 33.7 us -> 23.7 us  [the longest x1 14 us: per_device(): parts = lax.all_to_all(parts, seq, 0, 0, tiled=True)]
    pallas_call x0 -> x6, Pallas kernels: none -> 4.87 us  [the longest x1 1.53 us: per_device(): call(query_kernel, (devices, cols // 2, 2 * rows), [SMEM, HBM, HBM, HBM],...]
    slice x21 -> x0, local copies, waits for them, and re-layouts: 3.44 us -> none  [the longest x20 3.4 us: combined_pairwise(): part[side::2]]
    dot_general x6 -> x0, matrix products: 2.27 us -> none  [the longest x1 0.97 us: per_device(): jnp.einsum('btkn,kcn->btkc', query_nope, key_weight, preferred_element_ty...]
    ppermute x0 -> x4, waiting for transfers between devices: none -> 1.94 us  [exchange(): came = lax.ppermute(sent, 'run', [(i, i ^ step) for i in range(RUN)])]
    all_to_all x3 -> x0, other arithmetic: 1.76 us -> none  [the longest x1 0.95 us: sum_at_owner(): parts = lax.all_to_all(split_up(x, dim, length), axis, 0, 0, tiled=True)]
  transfers between devices with their start and end apart: 2 -> 6, of which waited for: 2 -> 4; matrix products, arithmetic and copies ran while one was open for 0% -> 0% of each run, Pallas kernels for 0% -> 3%
where the time goes in v1:
time: 105 us; the launch traced here: 104 us
  starting transfers between devices  40 us (38%)
  blocking collectives  28.7 us (27%)
  waiting for transfers between devices  25.7 us (24%)
  Pallas kernels  4.87 us (5%)
  local copies, waits for them, and re-layouts  3.69 us (4%)
    all_to_all x1, blocking collectives, per_device(): terms = lax.all_to_all(terms, seq, 0, 0, tiled=True)  19.7 us
    all_to_all x1, starting transfers between devices, per_device(): queries = lax.all_to_all(pieces, seq, 0, 0, tiled=True)  18.9 us
    ppermute x4, starting transfers between devices, exchange(): came = lax.ppermute(sent, 'run', [(i, i ^ step) for i in range(RUN)])  16.5 us
    all_to_all x1, waiting for transfers between devices, per_device(): parts = lax.all_to_all(parts, seq, 0, 0, tiled=True)  14 us
    all_to_all x1, waiting for transfers between devices, per_device(): queries = lax.all_to_all(pieces, seq, 0, 0, tiled=True)  9.72 us
    all_to_all x1, blocking collectives, per_device(): sums = lax.all_to_all(sums, 'heads', 0, 0, tiled=True)  8.98 us
    all_to_all x1, starting transfers between devices, per_device(): parts = lax.all_to_all(parts, seq, 0, 0, tiled=True)  4.57 us
    unnamed x18, local copies, waits for them, and re-layouts  3.65 us
  transfers between devices with their start and end apart: 6, of which 4 were waited for; matrix products, arithmetic and copies ran while one was open for 0% of the time, Pallas kernels for 3%

profile of v1, /device:TPU:1, one launch (start us, length us, event | category | flops | bytes accessed | tf_op | source)
XLA Modules:
  0.0 104.5 jit_solution(4020948100503626356)
XLA Ops:
  0.0 0.1 pad_add_fusion.place_ref
  0.1 0.8 copy-done.4
  0.9 0.7 copy-done.8
  1.6 0.6 shard_map.103
  2.2 5.7 %collective-permute-start = (bf16[1,8,8,128]{3,2,1,0:T(8,128)(2,1)S(1)}, bf16[1,8,8,128]{3,2,1,0:T(8,128)(2,1)S(1)}, u32[]{:S(2)}, u32[]{:S(2)}) collective-permute-start(bf16[1,8,8,128]{3,2,1,0:T(8,128)(2,1)S(1)} %get-tuple-element.16), channel_id=1, source_target_pairs={{0,8},{1,9},{2,10},{3,11},{4,12},{5,13},{6,14},{7,15},{8,0},{9,1},... | collective-permute-start | bytes 49160 | tf_op jit(solution)/shard_map/ppermute | solution.py:159
  7.9 1.1 %collective-permute-done = bf16[1,8,8,128]{3,2,1,0:T(8,128)(2,1)S(1)} collective-permute-done((bf16[1,8,8,128]{3,2,1,0:T(8,128)(2,1)S(1)}, bf16[1,8,8,128]{3,2,1,0:T(8,128)(2,1)S(1)}, u32[]{:S(2)}, u32[]{:S(2)}) %collective-permute-start) | collective-permute-done | bytes 16416 | tf_op jit(solution)/shard_map/ppermute | solution.py:159
  9.0 3.5 %collective-permute-start.1 = (bf16[2,4,8,128]{3,2,1,0:T(8,128)(2,1)S(1)}, bf16[2,4,8,128]{3,2,1,0:T(8,128)(2,1)S(1)}, u32[]{:S(2)}, u32[]{:S(2)}) collective-permute-start(bf16[2,4,8,128]{3,2,1,0:T(8,128)(2,1)S(1)} %get-tuple-element.14), channel_id=1, source_target_pairs={{0,4},{1,5},{2,6},{3,7},{4,0},{5,1},{6,2},{7,3},{8,12},{9,13},{10,... | collective-permute-start | bytes 49160 | tf_op jit(solution)/shard_map/ppermute | solution.py:159
  12.6 0.0 copy-start.3
  12.6 0.7 copy-done.3
  13.4 0.7 copy-done.5
  14.1 0.7 copy-done.7
  14.8 1.5 %shard_map.100 = bf16[64,4,128]{2,1,0:T(4,128)(2,1)} custom-call(s32[1]{0:T(128)} %bitcast.2.block_ref, f32[4,16]{1,0:T(4,128)S(1)} %bitcast.41, bf16[64,128]{1,0:T(8,128)(2,1)S(1)} %bitcast.39, bf16[16,8,128]{2,1,0:T(8,128)(2,1)S(1)} %copy-done.3), custom_call_target="tpu_custom_call" | custom-call | tf_op jit(solution)/shard_map/pallas_call | solution.py:191
  16.3 18.9 %all-to-all-start = ((bf16[64,4,128]{2,1,0:T(4,128)(2,1)}), bf16[64,4,128]{2,1,0:T(4,128)(2,1)S(1)}, u32[]{:S(2)}, u32[]{:S(2)}) async-start(bf16[64,4,128]{2,1,0:T(4,128)(2,1)} %shard_map.100), calls=%async_computation | async-start | bytes 131072 | tf_op jit(solution)/shard_map/all_to_all | solution.py:202
  35.2 0.0 collective-permute-done.1
  35.2 0.0 copy-start.2
  35.2 0.0 copy-start.6
  35.2 4.8 %collective-permute-start.2 = (bf16[4,2,8,128]{3,2,1,0:T(8,128)(2,1)S(1)}, bf16[4,2,8,128]{3,2,1,0:T(8,128)(2,1)S(1)}, u32[]{:S(2)}, u32[]{:S(2)}) collective-permute-start(bf16[4,2,8,128]{3,2,1,0:T(8,128)(2,1)S(1)} %get-tuple-element.12), channel_id=1, source_target_pairs={{0,2},{1,3},{2,0},{3,1},{4,6},{5,7},{6,4},{7,5},{8,10},{9,11},{10,... | collective-permute-start | bytes 49160 | tf_op jit(solution)/shard_map/ppermute | solution.py:159
  40.7 0.0 copy-done
  40.7 0.0 copy-done.2
  40.7 0.7 shard_map.101
  41.4 9.7 %all-to-all-done.refs_2_ = bf16[64,4,128]{2,1,0:T(4,128)(2,1)S(1)} async-done(((bf16[64,4,128]{2,1,0:T(4,128)(2,1)}), bf16[64,4,128]{2,1,0:T(4,128)(2,1)S(1)}, u32[]{:S(2)}, u32[]{:S(2)}) %all-to-all-start) | async-done | bytes 65568 | tf_op jit(solution)/shard_map/all_to_all | solution.py:202
  51.1 1.2 %shard_map.102 = bf16[64,3,2,128]{3,2,1,0:T(2,128)(2,1)} custom-call(s32[1]{0:T(128)S(6)} %copy.20.refs_0_, s32[1]{0:T(128)} %bitcast.1.refs_1_, bf16[64,4,128]{2,1,0:T(4,128)(2,1)S(1)} %all-to-all-done.refs_2_, f32[64,512]{1,0:T(8,128)S(1)} %get-tuple-element.7.refs_3_, bf16[512,512]{1,0:T(8,128)(2,1)S(1)} %get-tuple-element.8.refs_4_, ...), custom_call_target="tpu_custom_call" | custom-call | tf_op jit(solution)/shard_map/pallas_call | solution.py:213
  52.3 4.6 %all-to-all-start.1 = ((bf16[64,3,2,128]{3,2,1,0:T(2,128)(2,1)}), bf16[64,3,2,128]{3,2,1,0:T(2,128)(2,1)S(1)}, u32[]{:S(2)}, u32[]{:S(2)}) async-start(bf16[64,3,2,128]{3,2,1,0:T(2,128)(2,1)} %shard_map.102), calls=%async_computation.1 | async-start | bytes 196608 | tf_op jit(solution)/shard_map/all_to_all | solution.py:218
  56.9 0.0 collective-permute-done.2
  56.9 2.5 %collective-permute-start.3 = (bf16[8,1,8,128]{3,2,1,0:T(8,128)(2,1)S(1)}, bf16[8,1,8,128]{3,2,1,0:T(8,128)(2,1)S(1)}, u32[]{:S(2)}, u32[]{:S(2)}) collective-permute-start(bf16[8,1,8,128]{3,2,1,0:T(8,128)(2,1)S(1)} %get-tuple-element.10), channel_id=1, source_target_pairs={{0,1},{1,0},{2,3},{3,2},{4,5},{5,4},{6,7},{7,6},{8,9},{9,8},{10,11... | collective-permute-start | bytes 49160 | tf_op jit(solution)/shard_map/ppermute | solution.py:159
  59.4 0.8 collective-permute-done.3
  60.3 14.0 %all-to-all-done.1.parts_ref = bf16[64,3,2,128]{3,2,1,0:T(2,128)(2,1)S(1)} async-done(((bf16[64,3,2,128]{3,2,1,0:T(2,128)(2,1)}), bf16[64,3,2,128]{3,2,1,0:T(2,128)(2,1)S(1)}, u32[]{:S(2)}, u32[]{:S(2)}) %all-to-all-start.1) | async-done | bytes 98336 | tf_op jit(solution)/shard_map/all_to_all | solution.py:218
  74.3 0.7 shard_map.104
  74.9 19.7 %all_to_all.20.parts_ref = bf16[64,4,128]{2,1,0:T(4,128)(2,1)S(1)} all-to-all(bf16[64,4,128]{2,1,0:T(4,128)(2,1)S(1)} %shard_map.104), channel_id=1, replica_groups=mesh['heads'=8,'quarter'=4,'run'=16] {'quarter','run'}, dimensions={0} | all-to-all | bytes 131072 | tf_op jit(solution)/shard_map/all_to_all | solution.py:223
  94.7 0.2 shard_map.105
  94.9 9.0 %all_to_all.21 = f32[8,4,112]{2,1,0:T(4,128)S(1)} all-to-all(f32[8,4,112]{2,1,0:T(4,128)S(1)} %shard_map.105), channel_id=1, replica_groups=mesh['heads'=8,'quarter'=4,'run'=16] {'heads'}, dimensions={0} | all-to-all | bytes 28672 | tf_op jit(solution)/shard_map/all_to_all | solution.py:225
  103.9 0.6 reduce_sum.9
  (19 shorter events, 0.1 us)
Async XLA Ops:
  0.0 40.7 %copy-start = (bf16[1,512,512]{2,1,0:T(8,128)(2,1)S(1)}, bf16[1,512,512]{2,1,0:T(8,128)(2,1)}, u32[]{:S(2)}) copy-start(bf16[1,512,512]{2,1,0:T(8,128)(2,1)} %param.12) | copy-start | bytes 1572868
  0.1 0.8 copy-start.4
  0.9 0.7 copy-start.8
  2.2 6.8 %collective-permute-start = (bf16[1,8,8,128]{3,2,1,0:T(8,128)(2,1)S(1)}, bf16[1,8,8,128]{3,2,1,0:T(8,128)(2,1)S(1)}, u32[]{:S(2)}, u32[]{:S(2)}) collective-permute-start(bf16[1,8,8,128]{3,2,1,0:T(8,128)(2,1)S(1)} %get-tuple-element.16), channel_id=1, source_target_pairs={{0,8},{1,9},{2,10},{3,11},{4,12},{5,13},{6,14},{7,15},{8,0},{9,1},... | collective-permute-start | bytes 49160 | tf_op jit(solution)/shard_map/ppermute | solution.py:159
  9.0 26.1 %collective-permute-start.1 = (bf16[2,4,8,128]{3,2,1,0:T(8,128)(2,1)S(1)}, bf16[2,4,8,128]{3,2,1,0:T(8,128)(2,1)S(1)}, u32[]{:S(2)}, u32[]{:S(2)}) collective-permute-start(bf16[2,4,8,128]{3,2,1,0:T(8,128)(2,1)S(1)} %get-tuple-element.14), channel_id=1, source_target_pairs={{0,4},{1,5},{2,6},{3,7},{4,0},{5,1},{6,2},{7,3},{8,12},{9,13},{10,... | collective-permute-start | bytes 49160 | tf_op jit(solution)/shard_map/ppermute | solution.py:159
  12.6 0.8 copy-start.3
  13.4 0.7 copy-start.5
  14.1 0.7 copy-start.7
  16.3 34.8 %all-to-all-start = ((bf16[64,4,128]{2,1,0:T(4,128)(2,1)}), bf16[64,4,128]{2,1,0:T(4,128)(2,1)S(1)}, u32[]{:S(2)}, u32[]{:S(2)}) async-start(bf16[64,4,128]{2,1,0:T(4,128)(2,1)} %shard_map.100), calls=%async_computation | async-start | bytes 131072 | tf_op jit(solution)/shard_map/all_to_all | solution.py:202
  35.2 5.5 %copy-start.2 = (bf16[1,64,512]{2,1,0:T(8,128)(2,1)S(1)}, bf16[1,64,512]{2,1,0:T(8,128)(2,1)}, u32[]{:S(2)}) copy-start(bf16[1,64,512]{2,1,0:T(8,128)(2,1)} %param.13) | copy-start | bytes 196612
  35.2 5.5 %copy-start.6 = (bf16[1,4,16,64]{3,2,1,0:T(8,128)(2,1)S(1)}, bf16[1,4,16,64]{3,2,1,0:T(8,128)(2,1)}, u32[]{:S(2)}) copy-start(bf16[1,4,16,64]{3,2,1,0:T(8,128)(2,1)} %param.11) | copy-start | bytes 24580
  35.2 21.7 %collective-permute-start.2 = (bf16[4,2,8,128]{3,2,1,0:T(8,128)(2,1)S(1)}, bf16[4,2,8,128]{3,2,1,0:T(8,128)(2,1)S(1)}, u32[]{:S(2)}, u32[]{:S(2)}) collective-permute-start(bf16[4,2,8,128]{3,2,1,0:T(8,128)(2,1)S(1)} %get-tuple-element.12), channel_id=1, source_target_pairs={{0,2},{1,3},{2,0},{3,1},{4,6},{5,7},{6,4},{7,5},{8,10},{9,11},{10,... | collective-permute-start | bytes 49160 | tf_op jit(solution)/shard_map/ppermute | solution.py:159
  52.3 42.4 %copy-start.1 = (bf16[2048,112]{0,1:T(8,128)(2,1)S(1)}, bf16[2048,112]{0,1:T(8,128)(2,1)}, u32[]{:S(2)}) copy-start(bf16[2048,112]{0,1:T(8,128)(2,1)} %param.19) | copy-start | bytes 1376260
  52.3 22.0 %all-to-all-start.1 = ((bf16[64,3,2,128]{3,2,1,0:T(2,128)(2,1)}), bf16[64,3,2,128]{3,2,1,0:T(2,128)(2,1)S(1)}, u32[]{:S(2)}, u32[]{:S(2)}) async-start(bf16[64,3,2,128]{3,2,1,0:T(2,128)(2,1)} %shard_map.102), calls=%async_computation.1 | async-start | bytes 196608 | tf_op jit(solution)/shard_map/all_to_all | solution.py:218
  56.9 3.3 %collective-permute-start.3 = (bf16[8,1,8,128]{3,2,1,0:T(8,128)(2,1)S(1)}, bf16[8,1,8,128]{3,2,1,0:T(8,128)(2,1)S(1)}, u32[]{:S(2)}, u32[]{:S(2)}) collective-permute-start(bf16[8,1,8,128]{3,2,1,0:T(8,128)(2,1)S(1)} %get-tuple-element.10), channel_id=1, source_target_pairs={{0,1},{1,0},{2,3},{3,2},{4,5},{5,4},{6,7},{7,6},{8,9},{9,8},{10,11... | collective-permute-start | bytes 49160 | tf_op jit(solution)/shard_map/ppermute | solution.py:159

commit v2 on v1

v2 whole, which is shorter than its diff:
```python
import jax
import jax.numpy as jnp
from jax import lax
from jax.experimental import pallas as pl
from jax.experimental.pallas import tpu as pltpu
from jax.sharding import PartitionSpec as P

QB = 128
HEADS = 16
FIRST = 34
LANES = 128
NEG = -1e30
F32 = jnp.float32
BF16 = jnp.bfloat16
SMEM = pl.BlockSpec(memory_space=pltpu.SMEM)
HBM = pl.BlockSpec(memory_space=pltpu.HBM)
VMEM = pl.BlockSpec(memory_space=pltpu.VMEM)


def iota(shape, dim):
    return lax.broadcasted_iota(jnp.int32, shape, dim)


def dot(a, b, dims=((1,), (0,))):
    return lax.dot_general(a, b, (dims, ((), ())), preferred_element_type=F32)


def head_major(drafts, heads, copies):
    rows = drafts * heads
    col = iota((rows, copies * rows), 1) % rows
    source = (col % drafts) * heads + col // drafts
    return (iota((rows, copies * rows), 0) == source).astype(BF16)


def message_kernel(block_ref, *refs):
    sources, out_ref, targets, sems = refs[:5], refs[5], refs[6:11], refs[11]
    copies = [pltpu.make_async_copy(*pair, sems.at[k]) for k, pair in enumerate(zip(sources, targets))]
    for copy in copies:
        copy.start()
    for copy in copies:
        copy.wait()
    key_ref, query_ref, value_ref, key_scale_ref, value_scale_ref = targets
    heads, cols, width = key_ref.shape
    rows = query_ref.shape[0]
    block = block_ref[0]
    weight = jnp.concatenate(
        [(key_ref[h].astype(F32) * key_scale_ref[block, h]).astype(BF16) for h in range(heads)], axis=0
    )
    both = dot(weight, query_ref[...], ((1,), (1,)))
    own = iota(both.shape, 0) // cols == iota(both.shape, 1) % heads
    piece = jnp.sum(jnp.where(own, both, 0.0).reshape(heads, cols, rows), axis=0)
    moved = dot(piece.astype(BF16), head_major(rows // heads, heads, cols // 2))
    kept = jnp.where(iota(moved.shape, 0) // 2 == iota(moved.shape, 1) // rows, moved, 0.0)
    folded = sum(kept[i : i + 2] for i in range(0, cols, 2)).astype(BF16)
    for k in range(2):
        tile = folded[:, k * LANES : (k + 1) * LANES]
        out_ref[:, k] = jnp.broadcast_to(tile[None], (out_ref.shape[0], 2, LANES))
    for h in range(heads):
        weight = value_ref[h].astype(F32) * value_scale_ref[block, h]
        for q in range(cols // 2):
            out_ref[q * heads + h, 2] = weight[2 * q : 2 * q + 2].astype(BF16)


def ready_kernel(query_ref, key_ref, cache_ref, rope_ref, moved_ref):
    rows = query_ref.shape[0]
    latent = cache_ref.shape[1]
    query = dot(head_major(rows // HEADS, HEADS, 1), query_ref[...], ((0,), (0,))).astype(BF16)
    rope_ref[...] = dot(query, key_ref[...])
    new = iota((latent, latent), 1)
    quarter, sender, j = new // LANES, new % LANES // 2, new % 2
    source = (sender + FIRST) % (LANES // 2) * 8 + quarter * 2 + j
    order = (iota((latent, latent), 0) == source).astype(BF16)
    moved_ref[...] = dot(cache_ref[...], order).astype(BF16)


def split3(x):
    high = x.astype(BF16).astype(F32)
    middle = (x - high).astype(BF16).astype(F32)
    return high, middle, x - high - middle


def tile_of(ref, k):
    return ref[:, k].reshape(2 * ref.shape[0], LANES)


def attend_kernel(factor, length_ref, start_ref, queries_ref, rope_ref, cache_ref, out_ref):
    rows, positions = rope_ref.shape
    drafts = rows // HEADS
    tiles = [tile_of(queries_ref, k) for k in range(2)]
    queries = jnp.concatenate([tile[:, at : at + rows] for tile in tiles for at in (0, rows)], axis=0)
    scores = (dot(queries, cache_ref[...], ((0,), (1,))) + rope_ref[...]) * factor
    position = start_ref[0] + iota(scores.shape, 1)
    visible = position < length_ref[0] + iota(scores.shape, 0) % drafts
    top = jnp.max(jnp.where(visible, scores, NEG), axis=1, keepdims=True)
    probs = jnp.where(visible, jnp.exp(scores - top), 0.0)
    total = jnp.sum(probs, axis=1, keepdims=True)
    out = dot(probs.astype(BF16), cache_ref[...])
    lane = iota((rows, LANES), 1)
    stats = jnp.zeros(lane.shape, F32)
    for k, part in enumerate((*split3(top), *split3(total))):
        stats = jnp.where(lane % 8 == k, part, stats)
    low = iota((2, LANES), 1) < 8
    for h in range(HEADS):
        at = h * drafts
        both = jnp.where(low, stats[at : at + 2], stats[at + 2 : at + 4]).astype(BF16)
        for q in range(out_ref.shape[0] // HEADS):
            columns = slice(q * LANES, (q + 1) * LANES)
            for k in range(drafts // 2):
                out_ref[q * HEADS + h, k] = out[at + 2 * k : at + 2 * k + 2, columns].astype(BF16)
            out_ref[q * HEADS + h, drafts // 2] = both


def head_kernel(parts_ref, queries_ref, out_ref):
    pairs = parts_ref.shape[1] - 1
    stats = parts_ref[:, pairs].astype(F32)
    latents = []
    for k in range(pairs):
        tops, sums = (
            sum(stats[:, :, 8 * k + at + i : 8 * k + at + i + 1] for i in range(3)) for at in (0, 3)
        )
        shrink = jnp.exp(tops - jnp.max(tops, axis=0, keepdims=True))
        total = jnp.sum(sums * shrink, axis=0)
        merged = jnp.sum(parts_ref[:, k].astype(F32) * shrink, axis=0)
        latents.append(merged / total)
    latent = jnp.concatenate(latents, axis=0).astype(BF16)
    out_ref[...] = jnp.broadcast_to(dot(latent, tile_of(queries_ref, 2)).astype(BF16)[None], out_ref.shape)


def project_kernel(parts_ref, weight_ref, out_ref):
    devices = parts_ref.shape[0]
    heads = sum(parts_ref[at : at + HEADS].astype(F32) for at in range(0, devices, HEADS)).astype(BF16)
    flat = jnp.concatenate([heads[h] for h in range(HEADS)], axis=1)
    term = dot(flat, weight_ref[...], ((1,), (1,)))
    out_ref[...] = jnp.broadcast_to(term[None], out_ref.shape)


def call(kernel, shapes, specs, dtypes=BF16, scratch=(), limit=32 * 1024 * 1024):
    if isinstance(dtypes, tuple):
        out_shape = [jax.ShapeDtypeStruct(s, d) for s, d in zip(shapes, dtypes)]
        out_specs = [VMEM] * len(shapes)
    else:
        out_shape, out_specs = jax.ShapeDtypeStruct(shapes, dtypes), VMEM
    return pl.pallas_call(
        kernel,
        out_shape=out_shape,
        in_specs=specs,
        out_specs=out_specs,
        scratch_shapes=scratch,
        compiler_params=pltpu.CompilerParams(vmem_limit_bytes=limit),
    )


def to_everyone(x, axis, first):
    size = lax.axis_size(axis)
    order = [(first + k) % size for k in range(size)]
    return lax.all_to_all(x, axis, 0, 0, tiled=True, axis_index_groups=[order])


def per_device(
    query_nope,
    query_rope,
    latent_cache,
    rope_keys,
    lengths,
    key_quant,
    key_scale,
    value_quant,
    value_scale,
    out_weight,
):
    groups, devices = lax.axis_size("heads"), lax.axis_size("seq")
    _, drafts, heads, width = query_nope.shape
    rows = drafts * heads
    rope_width = query_rope.shape[3]
    _, positions, latent = latent_cache.shape
    cols = key_quant.shape[1]
    place = lax.axis_index("seq").astype(jnp.int32)
    block = (place * cols) >> 7
    start = place * positions
    factor = (width + rope_width) ** (-0.5)
    tiles = (devices, 3, 2, LANES)

    messages = call(
        message_kernel,
        tiles,
        [SMEM] + [HBM] * 5,
        scratch=(
            pltpu.VMEM(key_quant.shape, BF16),
            pltpu.VMEM((rows, width), BF16),
            pltpu.VMEM(value_quant.shape, BF16),
            pltpu.SMEM(key_scale.T.shape, F32),
            pltpu.SMEM(value_scale.T.shape, F32),
            pltpu.SemaphoreType.DMA((5,)),
        ),
        limit=None,
    )(block[None], key_quant, query_nope.reshape(rows, width), value_quant, key_scale.T, value_scale.T)
    queries = to_everyone(messages, "seq", FIRST)

    rope, moved = call(
        ready_kernel, ((rows, positions), (positions, latent)), [VMEM] * 3, (F32, BF16)
    )(query_rope.reshape(rows, rope_width), rope_keys[0], latent_cache[0])
    parts = call(lambda *refs: attend_kernel(factor, *refs), tiles, [SMEM, SMEM] + [VMEM] * 3)(
        lengths, start[None], queries, rope, moved
    )
    parts = to_everyone(parts, "seq", FIRST)

    terms = call(head_kernel, (devices, drafts, value_quant.shape[2]), [VMEM, VMEM])(parts, queries)
    terms = to_everyone(terms, "seq", FIRST)
    sums = call(project_kernel, (groups, drafts, out_weight.shape[1]), [VMEM, VMEM], F32)(
        terms, out_weight.T
    )
    sums = to_everyone(sums, "heads", 0)
    return jnp.sum(sums, axis=0).astype(BF16)[None]


def solution(mesh):
    in_specs = (
        P(None, None, "heads", None),
        P(None, None, "heads", None),
        P(None, "seq", None),
        P(None, None, "seq"),
        P(),
        P("heads", "seq", None),
        P("heads", None),
        P("heads", "seq", None),
        P("heads", None),
        P("heads", "seq"),
    )
    out_specs = P(None, None, "seq")
    return jax.shard_map(
        per_device, mesh=mesh, in_specs=in_specs, out_specs=out_specs, check_vma=False
    )
```

time: 105 us -> 83.6 us (0.80)
  waiting for transfers between devices: 25.7 us -> 3.17 us
  blocking collectives: 28.7 us -> 49.6 us
  starting transfers between devices: 40 us -> 23.4 us
  local copies, waits for them, and re-layouts: 3.69 us -> 1.06 us
    all_to_all x2 -> x3, blocking collectives: 28.7 us -> 49.6 us  [to_everyone(): return lax.all_to_all(x, axis, 0, 0, tiled=True, axis_index_groups=[order])]
    all_to_all x2 -> x1, waiting for transfers between devices: 23.7 us -> 3.17 us  [to_everyone(): return lax.all_to_all(x, axis, 0, 0, tiled=True, axis_index_groups=[order])]
    ppermute x4 -> x0, starting transfers between devices: 16.5 us -> none  [exchange(): came = lax.ppermute(sent, 'run', [(i, i ^ step) for i in range(RUN)])]
    unnamed x18 -> x8, local copies, waits for them, and re-layouts: 3.65 us -> 1.06 us
    ppermute x4 -> x0, waiting for transfers between devices: 1.94 us -> none  [exchange(): came = lax.ppermute(sent, 'run', [(i, i ^ step) for i in range(RUN)])]
    pallas_call x5 -> x4, Pallas kernels: 4.22 us -> 3.35 us  [the longest x1 1.84 us: per_device(): call(message_kernel, tiles, [SMEM] + [HBM] * 5, scratch=(pltpu.VMEM(key_q...]
    all_to_all x2 -> x1, starting transfers between devices: 23.4 us -> 23.4 us  [to_everyone(): return lax.all_to_all(x, axis, 0, 0, tiled=True, axis_index_groups=[order])]
  transfers between devices with their start and end apart: 6 -> 1, of which waited for: 4 -> 1; matrix products, arithmetic and copies ran while one was open for 0% -> 0% of each run, Pallas kernels for 3% -> 1%
where the time goes in v2:
time: 83.6 us; the launch traced here: 82.5 us
  blocking collectives  49.6 us (59%)
  starting transfers between devices  23.4 us (28%)
  Pallas kernels  4 us (5%)
  waiting for transfers between devices  3.17 us (4%)
  local copies, waits for them, and re-layouts  1.06 us (1%)
    all_to_all x3, blocking collectives, to_everyone(): return lax.all_to_all(x, axis, 0, 0, tiled=True, axis_index_groups=[order])  49.6 us
    all_to_all x1, starting transfers between devices, to_everyone(): return lax.all_to_all(x, axis, 0, 0, tiled=True, axis_index_groups=[order])  23.4 us
    all_to_all x1, waiting for transfers between devices, to_everyone(): return lax.all_to_all(x, axis, 0, 0, tiled=True, axis_index_groups=[order])  3.17 us
    pallas_call x1, Pallas kernels, per_device(): call(message_kernel, tiles, [SMEM] + [HBM] * 5, scratch=(pltpu.VMEM(key_q...  1.84 us
  transfers between devices with their start and end apart: 1, of which 1 were waited for; matrix products, arithmetic and copies ran while one was open for 0% of the time, Pallas kernels for 1%

profile of v2, /device:TPU:1, one launch (start us, length us, event | category | flops | bytes accessed | tf_op | source)
XLA Modules:
  0.0 82.5 jit_solution(3679091691998177498)
XLA Ops:
  0.0 1.8 %shard_map.100 = bf16[64,3,2,128]{3,2,1,0:T(2,128)(2,1)} custom-call(s32[1]{0:T(128)} %bitcast.1.block_ref, bf16[16,8,128]{2,1,0:T(8,128)(2,1)} %refs_0_.2, bf16[64,128]{1,0:T(8,128)(2,1)} %bitcast.16, bf16[16,8,128]{2,1,0:T(8,128)(2,1)} %refs_2_.1, f32[4,16]{1,0:T(4,128)} %bitcast.17, f32[4,16]{1,0:T(4,128)} %bitcast.18), custom_call_target="tpu_custom_call" | custom-call | tf_op jit(solution)/shard_map/pallas_call | solution.py:183
  1.8 0.0 copy-start.2
  1.9 0.0 copy-start.3
  1.9 23.4 %all-to-all-start = ((bf16[64,3,2,128]{3,2,1,0:T(2,128)(2,1)}), bf16[64,3,2,128]{3,2,1,0:T(2,128)(2,1)S(1)}, u32[]{:S(2)}, u32[]{:S(2)}) async-start(bf16[64,3,2,128]{3,2,1,0:T(2,128)(2,1)} %shard_map.100), calls=%async_computation | async-start | bytes 196608 | tf_op jit(solution)/shard_map/all_to_all | solution.py:156
  25.9 0.0 copy-done.2
  25.9 0.0 copy-done.3
  25.9 0.0 copy-start
  26.0 1.0 %copy-done = bf16[1,512,512]{2,1,0:T(8,128)(2,1)S(1)} copy-done((bf16[1,512,512]{2,1,0:T(8,128)(2,1)S(1)}, bf16[1,512,512]{2,1,0:T(8,128)(2,1)}, u32[]{:S(2)}) %copy-start) | copy-done | bytes 524312
  27.0 0.6 shard_map.101
  27.6 3.2 %all-to-all-done.refs_2_.queries_ref = bf16[64,3,2,128]{3,2,1,0:T(2,128)(2,1)S(1)} async-done(((bf16[64,3,2,128]{3,2,1,0:T(2,128)(2,1)}), bf16[64,3,2,128]{3,2,1,0:T(2,128)(2,1)S(1)}, u32[]{:S(2)}, u32[]{:S(2)}) %all-to-all-start) | async-done | bytes 98336 | tf_op jit(solution)/shard_map/all_to_all | solution.py:156
  30.8 0.6 shard_map.102
  31.5 0.0 copy-start.1
  31.5 20.7 %all_to_all.20.parts_ref = bf16[64,3,2,128]{3,2,1,0:T(2,128)(2,1)S(1)} all-to-all(bf16[64,3,2,128]{3,2,1,0:T(2,128)(2,1)S(1)} %shard_map.102), channel_id=1, replica_groups={{34,35,36,37,38,39,40,41,42,43,44,45,46,47,48,49,50,51,52,53,54,55,56,5..., dimensions={0} | all-to-all | bytes 196608 | tf_op jit(solution)/shard_map/all_to_all | solution.py:156
  52.2 0.6 shard_map.103
  52.9 19.2 %all_to_all.21.parts_ref = bf16[64,4,128]{2,1,0:T(4,128)(2,1)S(1)} all-to-all(bf16[64,4,128]{2,1,0:T(4,128)(2,1)S(1)} %shard_map.103), channel_id=1, replica_groups={{34,35,36,37,38,39,40,41,42,43,44,45,46,47,48,49,50,51,52,53,54,55,56,5..., dimensions={0} | all-to-all | bytes 131072 | tf_op jit(solution)/shard_map/all_to_all | solution.py:156
  72.1 0.0 copy-done.1
  72.1 0.2 shard_map.104
  72.3 9.7 %all_to_all.22 = f32[8,4,112]{2,1,0:T(4,128)S(1)} all-to-all(f32[8,4,112]{2,1,0:T(4,128)S(1)} %shard_map.104), channel_id=1, replica_groups={{0,64,128,192,256,320,384,448},{1,65,129,193,257,321,385,449},{2,66,130..., dimensions={0} | all-to-all | bytes 28672 | tf_op jit(solution)/shard_map/all_to_all | solution.py:156
  81.9 0.6 reduce_sum.9
Async XLA Ops:
  1.8 24.1 %copy-start.2 = (bf16[1,64,512]{2,1,0:T(8,128)(2,1)S(1)}, bf16[1,64,512]{2,1,0:T(8,128)(2,1)}, u32[]{:S(2)}) copy-start(bf16[1,64,512]{2,1,0:T(8,128)(2,1)} %param.13) | copy-start | bytes 196612
  1.9 24.1 %copy-start.3 = (bf16[1,4,16,64]{3,2,1,0:T(8,128)(2,1)S(1)}, bf16[1,4,16,64]{3,2,1,0:T(8,128)(2,1)}, u32[]{:S(2)}) copy-start(bf16[1,4,16,64]{3,2,1,0:T(8,128)(2,1)} %param.11) | copy-start | bytes 24580
  1.9 28.9 %all-to-all-start = ((bf16[64,3,2,128]{3,2,1,0:T(2,128)(2,1)}), bf16[64,3,2,128]{3,2,1,0:T(2,128)(2,1)S(1)}, u32[]{:S(2)}, u32[]{:S(2)}) async-start(bf16[64,3,2,128]{3,2,1,0:T(2,128)(2,1)} %shard_map.100), calls=%async_computation | async-start | bytes 196608 | tf_op jit(solution)/shard_map/all_to_all | solution.py:156
  25.9 1.0 %copy-start = (bf16[1,512,512]{2,1,0:T(8,128)(2,1)S(1)}, bf16[1,512,512]{2,1,0:T(8,128)(2,1)}, u32[]{:S(2)}) copy-start(bf16[1,512,512]{2,1,0:T(8,128)(2,1)} %param.12) | copy-start | bytes 1572868
  31.5 40.6 %copy-start.1 = (bf16[2048,112]{0,1:T(8,128)(2,1)S(1)}, bf16[2048,112]{0,1:T(8,128)(2,1)}, u32[]{:S(2)}) copy-start(bf16[2048,112]{0,1:T(8,128)(2,1)} %param.19) | copy-start | bytes 1376260

commit v3 on v2

--- a/solution.py
+++ b/solution.py
@@ -7,7 +7,8 @@
 
 QB = 128
 HEADS = 16
-FIRST = 34
+FIRST = 35
+LEADER = 5
 LANES = 128
 NEG = -1e30
 F32 = jnp.float32
@@ -32,7 +33,7 @@
     return (iota((rows, copies * rows), 0) == source).astype(BF16)
 
 
-def message_kernel(block_ref, *refs):
+def message_kernel(*refs):
     sources, out_ref, targets, sems = refs[:5], refs[5], refs[6:11], refs[11]
     copies = [pltpu.make_async_copy(*pair, sems.at[k]) for k, pair in enumerate(zip(sources, targets))]
     for copy in copies:
@@ -42,7 +43,7 @@
     key_ref, query_ref, value_ref, key_scale_ref, value_scale_ref = targets
     heads, cols, width = key_ref.shape
     rows = query_ref.shape[0]
-    block = block_ref[0]
+    block = lax.axis_index("seq") * cols // QB
     weight = jnp.concatenate(
         [(key_ref[h].astype(F32) * key_scale_ref[block, h]).astype(BF16) for h in range(heads)], axis=0
     )
@@ -83,13 +84,13 @@
     return ref[:, k].reshape(2 * ref.shape[0], LANES)
 
 
-def attend_kernel(factor, length_ref, start_ref, queries_ref, rope_ref, cache_ref, out_ref):
+def attend_kernel(factor, length_ref, queries_ref, rope_ref, cache_ref, out_ref):
     rows, positions = rope_ref.shape
     drafts = rows // HEADS
     tiles = [tile_of(queries_ref, k) for k in range(2)]
     queries = jnp.concatenate([tile[:, at : at + rows] for tile in tiles for at in (0, rows)], axis=0)
     scores = (dot(queries, cache_ref[...], ((0,), (1,))) + rope_ref[...]) * factor
-    position = start_ref[0] + iota(scores.shape, 1)
+    position = lax.axis_index("seq") * positions + iota(scores.shape, 1)
     visible = position < length_ref[0] + iota(scores.shape, 0) % drafts
     top = jnp.max(jnp.where(visible, scores, NEG), axis=1, keepdims=True)
     probs = jnp.where(visible, jnp.exp(scores - top), 0.0)
@@ -173,17 +174,13 @@
     rows = drafts * heads
     rope_width = query_rope.shape[3]
     _, positions, latent = latent_cache.shape
-    cols = key_quant.shape[1]
-    place = lax.axis_index("seq").astype(jnp.int32)
-    block = (place * cols) >> 7
-    start = place * positions
     factor = (width + rope_width) ** (-0.5)
     tiles = (devices, 3, 2, LANES)
 
     messages = call(
         message_kernel,
         tiles,
-        [SMEM] + [HBM] * 5,
+        [HBM] * 5,
         scratch=(
             pltpu.VMEM(key_quant.shape, BF16),
             pltpu.VMEM((rows, width), BF16),
@@ -193,14 +190,14 @@
             pltpu.SemaphoreType.DMA((5,)),
         ),
         limit=None,
-    )(block[None], key_quant, query_nope.reshape(rows, width), value_quant, key_scale.T, value_scale.T)
+    )(key_quant, query_nope.reshape(rows, width), value_quant, key_scale.T, value_scale.T)
     queries = to_everyone(messages, "seq", FIRST)
 
     rope, moved = call(
         ready_kernel, ((rows, positions), (positions, latent)), [VMEM] * 3, (F32, BF16)
     )(query_rope.reshape(rows, rope_width), rope_keys[0], latent_cache[0])
-    parts = call(lambda *refs: attend_kernel(factor, *refs), tiles, [SMEM, SMEM] + [VMEM] * 3)(
-        lengths, start[None], queries, rope, moved
+    parts = call(lambda *refs: attend_kernel(factor, *refs), tiles, [SMEM] + [VMEM] * 3)(
+        lengths, queries, rope, moved
     )
     parts = to_everyone(parts, "seq", FIRST)
 
@@ -209,7 +206,7 @@
     sums = call(project_kernel, (groups, drafts, out_weight.shape[1]), [VMEM, VMEM], F32)(
         terms, out_weight.T
     )
-    sums = to_everyone(sums, "heads", 0)
+    sums = to_everyone(sums, "heads", LEADER)
     return jnp.sum(sums, axis=0).astype(BF16)[None]
 
 

time: 83.6 us -> 80.4 us (0.962)
  blocking collectives: 49.6 us -> 47.1 us
    all_to_all x3, blocking collectives: 49.6 us -> 47.1 us  [to_everyone(): return lax.all_to_all(x, axis, 0, 0, tiled=True, axis_index_groups=[order])]
where the time goes in v3:
time: 80.4 us; the launch traced here: 79.7 us
  blocking collectives  47.1 us (59%)
  starting transfers between devices  23.1 us (29%)
  Pallas kernels  4.01 us (5%)
  waiting for transfers between devices  3.17 us (4%)
  local copies, waits for them, and re-layouts  1.06 us (1%)
    all_to_all x3, blocking collectives, to_everyone(): return lax.all_to_all(x, axis, 0, 0, tiled=True, axis_index_groups=[order])  47.1 us
    all_to_all x1, starting transfers between devices, to_everyone(): return lax.all_to_all(x, axis, 0, 0, tiled=True, axis_index_groups=[order])  23.1 us
    all_to_all x1, waiting for transfers between devices, to_everyone(): return lax.all_to_all(x, axis, 0, 0, tiled=True, axis_index_groups=[order])  3.17 us
    pallas_call x1, Pallas kernels, per_device(): call(message_kernel, tiles, [HBM] * 5, scratch=(pltpu.VMEM(key_quant.shap...  1.85 us
  transfers between devices with their start and end apart: 1, of which 1 were waited for; matrix products, arithmetic and copies ran while one was open for 0% of the time, Pallas kernels for 1%

profile of v3, /device:TPU:1, one launch (start us, length us, event | category | flops | bytes accessed | tf_op | source)
XLA Modules:
  0.0 79.7 jit_solution(7975242401500196819)
XLA Ops:
  0.0 1.9 %shard_map.100 = bf16[64,3,2,128]{3,2,1,0:T(2,128)(2,1)} custom-call(bf16[16,8,128]{2,1,0:T(8,128)(2,1)} %refs_0_.2, bf16[64,128]{1,0:T(8,128)(2,1)} %bitcast.14, bf16[16,8,128]{2,1,0:T(8,128)(2,1)} %refs_2_.1, f32[4,16]{1,0:T(4,128)} %bitcast.15, f32[4,16]{1,0:T(4,128)} %bitcast.16), custom_call_target="tpu_custom_call" | custom-call | tf_op jit(solution)/shard_map/pallas_call | solution.py:180
  1.9 0.0 copy-start.2
  1.9 0.0 copy-start.3
  1.9 23.1 %all-to-all-start = ((bf16[64,3,2,128]{3,2,1,0:T(2,128)(2,1)}), bf16[64,3,2,128]{3,2,1,0:T(2,128)(2,1)S(1)}, u32[]{:S(2)}, u32[]{:S(2)}) async-start(bf16[64,3,2,128]{3,2,1,0:T(2,128)(2,1)} %shard_map.100), calls=%async_computation | async-start | bytes 196608 | tf_op jit(solution)/shard_map/all_to_all | solution.py:157
  25.6 0.0 copy-done.2
  25.7 0.0 copy-done.3
  25.7 0.0 copy-start
  25.7 1.0 %copy-done = bf16[1,512,512]{2,1,0:T(8,128)(2,1)S(1)} copy-done((bf16[1,512,512]{2,1,0:T(8,128)(2,1)S(1)}, bf16[1,512,512]{2,1,0:T(8,128)(2,1)}, u32[]{:S(2)}) %copy-start) | copy-done | bytes 524312
  26.7 0.6 shard_map.101
  27.4 3.2 %all-to-all-done.refs_1_.queries_ref = bf16[64,3,2,128]{3,2,1,0:T(2,128)(2,1)S(1)} async-done(((bf16[64,3,2,128]{3,2,1,0:T(2,128)(2,1)}), bf16[64,3,2,128]{3,2,1,0:T(2,128)(2,1)S(1)}, u32[]{:S(2)}, u32[]{:S(2)}) %all-to-all-start) | async-done | bytes 98336 | tf_op jit(solution)/shard_map/all_to_all | solution.py:157
  30.5 0.6 shard_map.102
  31.2 0.0 copy-start.1
  31.2 20.5 %all_to_all.20.parts_ref = bf16[64,3,2,128]{3,2,1,0:T(2,128)(2,1)S(1)} all-to-all(bf16[64,3,2,128]{3,2,1,0:T(2,128)(2,1)S(1)} %shard_map.102), channel_id=1, replica_groups={{35,36,37,38,39,40,41,42,43,44,45,46,47,48,49,50,51,52,53,54,55,56,57,5..., dimensions={0} | all-to-all | bytes 196608 | tf_op jit(solution)/shard_map/all_to_all | solution.py:157
  51.7 0.6 shard_map.103
  52.3 18.9 %all_to_all.21.parts_ref = bf16[64,4,128]{2,1,0:T(4,128)(2,1)S(1)} all-to-all(bf16[64,4,128]{2,1,0:T(4,128)(2,1)S(1)} %shard_map.103), channel_id=1, replica_groups={{35,36,37,38,39,40,41,42,43,44,45,46,47,48,49,50,51,52,53,54,55,56,57,5..., dimensions={0} | all-to-all | bytes 131072 | tf_op jit(solution)/shard_map/all_to_all | solution.py:157
  71.2 0.0 copy-done.1
  71.2 0.2 shard_map.104
  71.4 7.7 %all_to_all.22 = f32[8,4,112]{2,1,0:T(4,128)S(1)} all-to-all(f32[8,4,112]{2,1,0:T(4,128)S(1)} %shard_map.104), channel_id=1, replica_groups={{320,384,448,0,64,128,192,256},{321,385,449,1,65,129,193,257},{322,386,..., dimensions={0} | all-to-all | bytes 28672 | tf_op jit(solution)/shard_map/all_to_all | solution.py:157
  79.2 0.6 reduce_sum.9
Async XLA Ops:
  1.9 23.8 %copy-start.2 = (bf16[1,64,512]{2,1,0:T(8,128)(2,1)S(1)}, bf16[1,64,512]{2,1,0:T(8,128)(2,1)}, u32[]{:S(2)}) copy-start(bf16[1,64,512]{2,1,0:T(8,128)(2,1)} %param.13) | copy-start | bytes 196612
  1.9 23.8 %copy-start.3 = (bf16[1,4,16,64]{3,2,1,0:T(8,128)(2,1)S(1)}, bf16[1,4,16,64]{3,2,1,0:T(8,128)(2,1)}, u32[]{:S(2)}) copy-start(bf16[1,4,16,64]{3,2,1,0:T(8,128)(2,1)} %param.11) | copy-start | bytes 24580
  1.9 28.7 %all-to-all-start = ((bf16[64,3,2,128]{3,2,1,0:T(2,128)(2,1)}), bf16[64,3,2,128]{3,2,1,0:T(2,128)(2,1)S(1)}, u32[]{:S(2)}, u32[]{:S(2)}) async-start(bf16[64,3,2,128]{3,2,1,0:T(2,128)(2,1)} %shard_map.100), calls=%async_computation | async-start | bytes 196608 | tf_op jit(solution)/shard_map/all_to_all | solution.py:157
  25.7 1.0 %copy-start = (bf16[1,512,512]{2,1,0:T(8,128)(2,1)S(1)}, bf16[1,512,512]{2,1,0:T(8,128)(2,1)}, u32[]{:S(2)}) copy-start(bf16[1,512,512]{2,1,0:T(8,128)(2,1)} %param.12) | copy-start | bytes 1572868
  31.2 40.0 %copy-start.1 = (bf16[2048,112]{0,1:T(8,128)(2,1)S(1)}, bf16[2048,112]{0,1:T(8,128)(2,1)}, u32[]{:S(2)}) copy-start(bf16[2048,112]{0,1:T(8,128)(2,1)} %param.19) | copy-start | bytes 1376260

commit v4 on v3

--- a/solution.py
+++ b/solution.py
@@ -7,7 +7,8 @@
 
 QB = 128
 HEADS = 16
-FIRST = 35
+FIRST = 34
+AHEAD = 1
 LEADER = 5
 LANES = 128
 NEG = -1e30
@@ -24,6 +25,14 @@
 
 def dot(a, b, dims=((1,), (0,))):
     return lax.dot_general(a, b, (dims, ((), ())), preferred_element_type=F32)
+
+
+def place_of(quarter, head):
+    return quarter * HEADS + head % (HEADS // 2) * 2 + head // (HEADS // 2)
+
+
+def turn_of(quarter, head, devices):
+    return (place_of(quarter, head) - AHEAD) % devices
 
 
 def head_major(drafts, heads, copies):
@@ -59,7 +68,7 @@
     for h in range(heads):
         weight = value_ref[h].astype(F32) * value_scale_ref[block, h]
         for q in range(cols // 2):
-            out_ref[q * heads + h, 2] = weight[2 * q : 2 * q + 2].astype(BF16)
+            out_ref[turn_of(q, h, out_ref.shape[0]), 2] = weight[2 * q : 2 * q + 2].astype(BF16)
 
 
 def ready_kernel(query_ref, key_ref, cache_ref, rope_ref, moved_ref):
@@ -69,7 +78,7 @@
     rope_ref[...] = dot(query, key_ref[...])
     new = iota((latent, latent), 1)
     quarter, sender, j = new // LANES, new % LANES // 2, new % 2
-    source = (sender + FIRST) % (LANES // 2) * 8 + quarter * 2 + j
+    source = (sender + FIRST + AHEAD) % (LANES // 2) * 8 + quarter * 2 + j
     order = (iota((latent, latent), 0) == source).astype(BF16)
     moved_ref[...] = dot(cache_ref[...], order).astype(BF16)
 
@@ -106,9 +115,10 @@
         both = jnp.where(low, stats[at : at + 2], stats[at + 2 : at + 4]).astype(BF16)
         for q in range(out_ref.shape[0] // HEADS):
             columns = slice(q * LANES, (q + 1) * LANES)
+            turn = turn_of(q, h, out_ref.shape[0])
             for k in range(drafts // 2):
-                out_ref[q * HEADS + h, k] = out[at + 2 * k : at + 2 * k + 2, columns].astype(BF16)
-            out_ref[q * HEADS + h, drafts // 2] = both
+                out_ref[turn, k] = out[at + 2 * k : at + 2 * k + 2, columns].astype(BF16)
+            out_ref[turn, drafts // 2] = both
 
 
 def head_kernel(parts_ref, queries_ref, out_ref):
@@ -127,12 +137,19 @@
     out_ref[...] = jnp.broadcast_to(dot(latent, tile_of(queries_ref, 2)).astype(BF16)[None], out_ref.shape)
 
 
-def project_kernel(parts_ref, weight_ref, out_ref):
-    devices = parts_ref.shape[0]
-    heads = sum(parts_ref[at : at + HEADS].astype(F32) for at in range(0, devices, HEADS)).astype(BF16)
-    flat = jnp.concatenate([heads[h] for h in range(HEADS)], axis=1)
-    term = dot(flat, weight_ref[...], ((1,), (1,)))
-    out_ref[...] = jnp.broadcast_to(term[None], out_ref.shape)
+def project_kernel(parts_ref, mine_ref, other_ref, out_ref):
+    place = lax.axis_index("seq")
+    half, core = (place + FIRST) % 2, place % 2
+    count = HEADS // 2
+    heads = sum(parts_ref[at : at + count].astype(F32) for at in range(0, parts_ref.shape[0], count)).astype(BF16)
+    flat = jnp.concatenate([heads[h] for h in range(count)], axis=1)
+    width = flat.shape[1]
+    rows = pl.ds(pl.multiple_of(half * width, width), width)
+    mine, other = (dot(flat, weight, ((1,), (1,))) for weight in (mine_ref[:, rows], other_ref[...]))
+    for to in range(2):
+        term = jnp.where(core == to, mine, other)
+        for g in range(out_ref.shape[0] // 2):
+            out_ref[2 * g + to] = term
 
 
 def call(kernel, shapes, specs, dtypes=BF16, scratch=(), limit=32 * 1024 * 1024):
@@ -151,10 +168,19 @@
     )
 
 
-def to_everyone(x, axis, first):
-    size = lax.axis_size(axis)
-    order = [(first + k) % size for k in range(size)]
-    return lax.all_to_all(x, axis, 0, 0, tiled=True, axis_index_groups=[order])
+def seq_order(devices, first, step=1):
+    return [[(first + k) % devices for k in range(at, devices, step)] for at in range(step)]
+
+
+def plane_order(groups, devices):
+    return [
+        [(LEADER + g) % groups * devices + at + core for g in range(groups) for core in range(2)]
+        for at in range(0, devices, 2)
+    ]
+
+
+def to_everyone(x, axis, order):
+    return lax.all_to_all(x, axis, 0, 0, tiled=True, axis_index_groups=order)
 
 
 def per_device(
@@ -191,22 +217,27 @@
         ),
         limit=None,
     )(key_quant, query_nope.reshape(rows, width), value_quant, key_scale.T, value_scale.T)
-    queries = to_everyone(messages, "seq", FIRST)
+    queries = to_everyone(messages, "seq", seq_order(devices, FIRST + AHEAD))
 
     rope, moved = call(
         ready_kernel, ((rows, positions), (positions, latent)), [VMEM] * 3, (F32, BF16)
     )(query_rope.reshape(rows, rope_width), rope_keys[0], latent_cache[0])
+    mine, _ = lax.optimization_barrier((out_weight.T, rope))
+    width = mine.shape[1] // 2
+    mine = lax.dynamic_slice_in_dim(mine, (lax.axis_index("seq") + 1 + FIRST) % 2 * width, width, 1)
+    other = lax.ppermute(mine, "seq", [(i, i ^ 1) for i in range(devices)])
     parts = call(lambda *refs: attend_kernel(factor, *refs), tiles, [SMEM] + [VMEM] * 3)(
         lengths, queries, rope, moved
     )
-    parts = to_everyone(parts, "seq", FIRST)
-
-    terms = call(head_kernel, (devices, drafts, value_quant.shape[2]), [VMEM, VMEM])(parts, queries)
-    terms = to_everyone(terms, "seq", FIRST)
-    sums = call(project_kernel, (groups, drafts, out_weight.shape[1]), [VMEM, VMEM], F32)(
-        terms, out_weight.T
-    )
-    sums = to_everyone(sums, "heads", LEADER)
+    parts, other = lax.optimization_barrier((parts, other))
+    parts = to_everyone(parts, "seq", seq_order(devices, FIRST + AHEAD))
+
+    terms = call(head_kernel, (devices // 2, drafts, value_quant.shape[2]), [VMEM, VMEM])(parts, queries)
+    terms = to_everyone(terms, "seq", seq_order(devices, FIRST, 2))
+    sums = call(project_kernel, (2 * groups, drafts, out_weight.shape[1]), [VMEM] * 3, F32)(
+        terms, out_weight.T, other
+    )
+    sums = to_everyone(sums, ("heads", "seq"), plane_order(groups, devices))
     return jnp.sum(sums, axis=0).astype(BF16)[None]
 
 

time: 80.4 us -> 79.4 us (0.988)
  waiting for transfers between devices: 3.17 us -> 0.84 us
  starting transfers between devices: 23.1 us -> 25.4 us
    all_to_all x1, waiting for transfers between devices: 3.17 us -> 0.84 us  [to_everyone(): return lax.all_to_all(x, axis, 0, 0, tiled=True, axis_index_groups=order)]
    ppermute x0 -> x1, starting transfers between devices: none -> 2.27 us  [per_device(): other = lax.ppermute(mine, 'seq', [(i, i ^ 1) for i in range(devices)])]
  transfers between devices with their start and end apart: 1 -> 2, of which waited for: 1 -> 1; matrix products, arithmetic and copies ran while one was open for 0% -> 0% of each run, Pallas kernels for 1% -> 2%
where the time goes in v4:
time: 79.4 us; the launch traced here: 79 us
  blocking collectives  46.4 us (58%)
  starting transfers between devices  25.4 us (32%)
  Pallas kernels  3.99 us (5%)
  local copies, waits for them, and re-layouts  1.07 us (1%)
  waiting for transfers between devices  0.84 us (1%)
    all_to_all x3, blocking collectives, to_everyone(): return lax.all_to_all(x, axis, 0, 0, tiled=True, axis_index_groups=order)  46.4 us
    all_to_all x1, starting transfers between devices, to_everyone(): return lax.all_to_all(x, axis, 0, 0, tiled=True, axis_index_groups=order)  23.1 us
    ppermute x1, starting transfers between devices, per_device(): other = lax.ppermute(mine, 'seq', [(i, i ^ 1) for i in range(devices)])  2.27 us
    pallas_call x1, Pallas kernels, per_device(): call(message_kernel, tiles, [HBM] * 5, scratch=(pltpu.VMEM(key_quant.shap...  1.85 us
  transfers between devices with their start and end apart: 2, of which 1 were waited for; matrix products, arithmetic and copies ran while one was open for 0% of the time, Pallas kernels for 2%

profile of v4, /device:TPU:1, one launch (start us, length us, event | category | flops | bytes accessed | tf_op | source)
XLA Modules:
  0.0 79.0 jit_solution(9738494106217779641)
XLA Ops:
  0.0 0.0 copy-start.2
  0.0 0.0 copy-start.3
  0.0 1.8 %shard_map.100 = bf16[64,3,2,128]{3,2,1,0:T(2,128)(2,1)} custom-call(bf16[16,8,128]{2,1,0:T(8,128)(2,1)} %refs_0_.2, bf16[64,128]{1,0:T(8,128)(2,1)} %bitcast.15, bf16[16,8,128]{2,1,0:T(8,128)(2,1)} %refs_2_.1, f32[4,16]{1,0:T(4,128)} %bitcast.16, f32[4,16]{1,0:T(4,128)} %bitcast.17), custom_call_target="tpu_custom_call" | custom-call | tf_op jit(solution)/shard_map/pallas_call | solution.py:206
  1.9 0.0 copy-start
  1.9 23.1 %all-to-all-start = ((bf16[64,3,2,128]{3,2,1,0:T(2,128)(2,1)}), bf16[64,3,2,128]{3,2,1,0:T(2,128)(2,1)S(1)}, u32[]{:S(2)}, u32[]{:S(2)}) async-start(bf16[64,3,2,128]{3,2,1,0:T(2,128)(2,1)} %shard_map.100), calls=%async_computation | async-start | bytes 196608 | tf_op jit(solution)/shard_map/all_to_all | solution.py:183
  25.0 0.0 copy-done.2
  25.0 0.0 copy-done.3
  25.0 0.0 copy-start.1
  25.0 1.0 %copy-done.1 = bf16[1,512,512]{2,1,0:T(8,128)(2,1)S(1)} copy-done((bf16[1,512,512]{2,1,0:T(8,128)(2,1)S(1)}, bf16[1,512,512]{2,1,0:T(8,128)(2,1)}, u32[]{:S(2)}) %copy-start.1) | copy-done | bytes 524312
  26.1 0.6 shard_map.101
  26.7 0.0 copy-done
  26.8 2.3 %collective-permute-start = (bf16[112,1024]{1,0:T(8,128)(2,1)S(1)}, bf16[112,1024]{1,0:T(8,128)(2,1)S(1)}, u32[]{:S(2)}, u32[]{:S(2)}) collective-permute-start(bf16[112,1024]{1,0:T(8,128)(2,1)S(1)} %constant_dynamic-slice_fusion), channel_id=1, source_target_pairs={{0,1},{1,0},{2,3},{3,2},{4,5},{5,4},{6,7},{7,6},{8,9},{9,8},{10,11... | collective-permute-start | bytes 688136 | tf_op jit(solution)/shard_map/ppermute | solution.py:228
  29.7 0.8 %all-to-all-done.refs_1_.queries_ref = bf16[64,3,2,128]{3,2,1,0:T(2,128)(2,1)S(1)} async-done(((bf16[64,3,2,128]{3,2,1,0:T(2,128)(2,1)}), bf16[64,3,2,128]{3,2,1,0:T(2,128)(2,1)S(1)}, u32[]{:S(2)}, u32[]{:S(2)}) %all-to-all-start) | async-done | bytes 98336 | tf_op jit(solution)/shard_map/all_to_all | solution.py:183
  30.5 0.6 shard_map.102
  31.2 0.0 collective-permute-done.other_ref
  31.2 20.3 %all_to_all.20.parts_ref = bf16[64,3,2,128]{3,2,1,0:T(2,128)(2,1)S(1)} all-to-all(bf16[64,3,2,128]{3,2,1,0:T(2,128)(2,1)S(1)} %shard_map.102), channel_id=1, replica_groups={{35,36,37,38,39,40,41,42,43,44,45,46,47,48,49,50,51,52,53,54,55,56,57,5..., dimensions={0} | all-to-all | bytes 196608 | tf_op jit(solution)/shard_map/all_to_all | solution.py:183
  51.5 0.6 shard_map.103
  52.1 16.2 %all_to_all.21.parts_ref = bf16[32,4,128]{2,1,0:T(4,128)(2,1)S(1)} all-to-all(bf16[32,4,128]{2,1,0:T(4,128)(2,1)S(1)} %shard_map.103), channel_id=1, replica_groups={{34,36,38,40,42,44,46,48,50,52,54,56,58,60,62,0,2,4,6,8,10,12,14,16,18,..., dimensions={0} | all-to-all | bytes 65536 | tf_op jit(solution)/shard_map/all_to_all | solution.py:183
  68.3 0.2 shard_map.104
  68.6 9.9 %all_to_all.22 = f32[16,4,112]{2,1,0:T(4,128)S(1)} all-to-all(f32[16,4,112]{2,1,0:T(4,128)S(1)} %shard_map.104), channel_id=1, replica_groups={{320,321,384,385,448,449,0,1,64,65,128,129,192,193,256,257},{322,323,38..., dimensions={0} | all-to-all | bytes 57344 | tf_op jit(solution)/shard_map/all_to_all | solution.py:183
  78.5 0.6 reduce_sum.9
  (1 shorter events, 0.0 us)
Async XLA Ops:
  0.0 25.0 %copy-start.2 = (bf16[1,64,512]{2,1,0:T(8,128)(2,1)S(1)}, bf16[1,64,512]{2,1,0:T(8,128)(2,1)}, u32[]{:S(2)}) copy-start(bf16[1,64,512]{2,1,0:T(8,128)(2,1)} %param.13) | copy-start | bytes 196612
  0.0 25.0 %copy-start.3 = (bf16[1,4,16,64]{3,2,1,0:T(8,128)(2,1)S(1)}, bf16[1,4,16,64]{3,2,1,0:T(8,128)(2,1)}, u32[]{:S(2)}) copy-start(bf16[1,4,16,64]{3,2,1,0:T(8,128)(2,1)} %param.11) | copy-start | bytes 24580
  1.9 24.9 %copy-start = (bf16[2048,112]{0,1:T(8,128)(2,1)S(1)}, bf16[2048,112]{0,1:T(8,128)(2,1)}, u32[]{:S(2)}) copy-start(bf16[2048,112]{0,1:T(8,128)(2,1)} %param.19) | copy-start | bytes 1376260
  1.9 28.7 %all-to-all-start = ((bf16[64,3,2,128]{3,2,1,0:T(2,128)(2,1)}), bf16[64,3,2,128]{3,2,1,0:T(2,128)(2,1)S(1)}, u32[]{:S(2)}, u32[]{:S(2)}) async-start(bf16[64,3,2,128]{3,2,1,0:T(2,128)(2,1)} %shard_map.100), calls=%async_computation | async-start | bytes 196608 | tf_op jit(solution)/shard_map/all_to_all | solution.py:183
  25.0 1.0 %copy-start.1 = (bf16[1,512,512]{2,1,0:T(8,128)(2,1)S(1)}, bf16[1,512,512]{2,1,0:T(8,128)(2,1)}, u32[]{:S(2)}) copy-start(bf16[1,512,512]{2,1,0:T(8,128)(2,1)} %param.12) | copy-start | bytes 1572868
  26.8 4.4 %collective-permute-start = (bf16[112,1024]{1,0:T(8,128)(2,1)S(1)}, bf16[112,1024]{1,0:T(8,128)(2,1)S(1)}, u32[]{:S(2)}, u32[]{:S(2)}) collective-permute-start(bf16[112,1024]{1,0:T(8,128)(2,1)S(1)} %constant_dynamic-slice_fusion), channel_id=1, source_target_pairs={{0,1},{1,0},{2,3},{3,2},{4,5},{5,4},{6,7},{7,6},{8,9},{9,8},{10,11... | collective-permute-start | bytes 688136 | tf_op jit(solution)/shard_map/ppermute | solution.py:228

commit v5 on v4

--- a/solution.py
+++ b/solution.py
@@ -149,7 +149,7 @@
     for to in range(2):
         term = jnp.where(core == to, mine, other)
         for g in range(out_ref.shape[0] // 2):
-            out_ref[2 * g + to] = term
+            out_ref[2 * g + 1 - to] = term
 
 
 def call(kernel, shapes, specs, dtypes=BF16, scratch=(), limit=32 * 1024 * 1024):
@@ -174,7 +174,7 @@
 
 def plane_order(groups, devices):
     return [
-        [(LEADER + g) % groups * devices + at + core for g in range(groups) for core in range(2)]
+        [(LEADER + g) % groups * devices + at + core for g in range(groups) for core in (1, 0)]
         for at in range(0, devices, 2)
     ]
 

time: 79.4 us -> 79.1 us (level)
  no operation moved by 1% of the time
where the time goes in v5:
time: 79.1 us; the launch traced here: 78.7 us
  blocking collectives  46.1 us (58%)
  starting transfers between devices  25.4 us (32%)
  Pallas kernels  3.99 us (5%)
  local copies, waits for them, and re-layouts  1.07 us (1%)
  waiting for transfers between devices  0.84 us (1%)
    all_to_all x3, blocking collectives, to_everyone(): return lax.all_to_all(x, axis, 0, 0, tiled=True, axis_index_groups=order)  46.1 us
    all_to_all x1, starting transfers between devices, to_everyone(): return lax.all_to_all(x, axis, 0, 0, tiled=True, axis_index_groups=order)  23.1 us
    ppermute x1, starting transfers between devices, per_device(): other = lax.ppermute(mine, 'seq', [(i, i ^ 1) for i in range(devices)])  2.27 us
    pallas_call x1, Pallas kernels, per_device(): call(message_kernel, tiles, [HBM] * 5, scratch=(pltpu.VMEM(key_quant.shap...  1.85 us
  transfers between devices with their start and end apart: 2, of which 1 were waited for; matrix products, arithmetic and copies ran while one was open for 0% of the time, Pallas kernels for 2%

profile of v5, /device:TPU:1, one launch (start us, length us, event | category | flops | bytes accessed | tf_op | source)
XLA Modules:
  0.0 78.7 jit_solution(10563608154625985278)
XLA Ops:
  0.0 0.0 copy-start.2
  0.0 0.0 copy-start.3
  0.0 1.8 %shard_map.100 = bf16[64,3,2,128]{3,2,1,0:T(2,128)(2,1)} custom-call(bf16[16,8,128]{2,1,0:T(8,128)(2,1)} %refs_0_.2, bf16[64,128]{1,0:T(8,128)(2,1)} %bitcast.15, bf16[16,8,128]{2,1,0:T(8,128)(2,1)} %refs_2_.1, f32[4,16]{1,0:T(4,128)} %bitcast.16, f32[4,16]{1,0:T(4,128)} %bitcast.17), custom_call_target="tpu_custom_call" | custom-call | tf_op jit(solution)/shard_map/pallas_call | solution.py:206
  1.9 0.0 copy-start
  1.9 23.1 %all-to-all-start = ((bf16[64,3,2,128]{3,2,1,0:T(2,128)(2,1)}), bf16[64,3,2,128]{3,2,1,0:T(2,128)(2,1)S(1)}, u32[]{:S(2)}, u32[]{:S(2)}) async-start(bf16[64,3,2,128]{3,2,1,0:T(2,128)(2,1)} %shard_map.100), calls=%async_computation | async-start | bytes 196608 | tf_op jit(solution)/shard_map/all_to_all | solution.py:183
  25.0 0.0 copy-done.2
  25.0 0.0 copy-done.3
  25.0 0.0 copy-start.1
  25.0 1.0 %copy-done.1 = bf16[1,512,512]{2,1,0:T(8,128)(2,1)S(1)} copy-done((bf16[1,512,512]{2,1,0:T(8,128)(2,1)S(1)}, bf16[1,512,512]{2,1,0:T(8,128)(2,1)}, u32[]{:S(2)}) %copy-start.1) | copy-done | bytes 524312
  26.1 0.6 shard_map.101
  26.7 0.0 copy-done
  26.8 2.3 %collective-permute-start = (bf16[112,1024]{1,0:T(8,128)(2,1)S(1)}, bf16[112,1024]{1,0:T(8,128)(2,1)S(1)}, u32[]{:S(2)}, u32[]{:S(2)}) collective-permute-start(bf16[112,1024]{1,0:T(8,128)(2,1)S(1)} %constant_dynamic-slice_fusion), channel_id=1, source_target_pairs={{0,1},{1,0},{2,3},{3,2},{4,5},{5,4},{6,7},{7,6},{8,9},{9,8},{10,11... | collective-permute-start | bytes 688136 | tf_op jit(solution)/shard_map/ppermute | solution.py:228
  29.7 0.8 %all-to-all-done.refs_1_.queries_ref = bf16[64,3,2,128]{3,2,1,0:T(2,128)(2,1)S(1)} async-done(((bf16[64,3,2,128]{3,2,1,0:T(2,128)(2,1)}), bf16[64,3,2,128]{3,2,1,0:T(2,128)(2,1)S(1)}, u32[]{:S(2)}, u32[]{:S(2)}) %all-to-all-start) | async-done | bytes 98336 | tf_op jit(solution)/shard_map/all_to_all | solution.py:183
  30.5 0.6 shard_map.102
  31.2 0.0 collective-permute-done.other_ref
  31.2 20.3 %all_to_all.20.parts_ref = bf16[64,3,2,128]{3,2,1,0:T(2,128)(2,1)S(1)} all-to-all(bf16[64,3,2,128]{3,2,1,0:T(2,128)(2,1)S(1)} %shard_map.102), channel_id=1, replica_groups={{35,36,37,38,39,40,41,42,43,44,45,46,47,48,49,50,51,52,53,54,55,56,57,5..., dimensions={0} | all-to-all | bytes 196608 | tf_op jit(solution)/shard_map/all_to_all | solution.py:183
  51.5 0.6 shard_map.103
  52.1 16.2 %all_to_all.21.parts_ref = bf16[32,4,128]{2,1,0:T(4,128)(2,1)S(1)} all-to-all(bf16[32,4,128]{2,1,0:T(4,128)(2,1)S(1)} %shard_map.103), channel_id=1, replica_groups={{34,36,38,40,42,44,46,48,50,52,54,56,58,60,62,0,2,4,6,8,10,12,14,16,18,..., dimensions={0} | all-to-all | bytes 65536 | tf_op jit(solution)/shard_map/all_to_all | solution.py:183
  68.3 0.2 shard_map.104
  68.6 9.6 %all_to_all.22 = f32[16,4,112]{2,1,0:T(4,128)S(1)} all-to-all(f32[16,4,112]{2,1,0:T(4,128)S(1)} %shard_map.104), channel_id=1, replica_groups={{321,320,385,384,449,448,1,0,65,64,129,128,193,192,257,256},{323,322,38..., dimensions={0} | all-to-all | bytes 57344 | tf_op jit(solution)/shard_map/all_to_all | solution.py:183
  78.1 0.6 reduce_sum.9
  (1 shorter events, 0.0 us)
Async XLA Ops:
  0.0 25.0 %copy-start.2 = (bf16[1,64,512]{2,1,0:T(8,128)(2,1)S(1)}, bf16[1,64,512]{2,1,0:T(8,128)(2,1)}, u32[]{:S(2)}) copy-start(bf16[1,64,512]{2,1,0:T(8,128)(2,1)} %param.13) | copy-start | bytes 196612
  0.0 25.0 %copy-start.3 = (bf16[1,4,16,64]{3,2,1,0:T(8,128)(2,1)S(1)}, bf16[1,4,16,64]{3,2,1,0:T(8,128)(2,1)}, u32[]{:S(2)}) copy-start(bf16[1,4,16,64]{3,2,1,0:T(8,128)(2,1)} %param.11) | copy-start | bytes 24580
  1.9 24.9 %copy-start = (bf16[2048,112]{0,1:T(8,128)(2,1)S(1)}, bf16[2048,112]{0,1:T(8,128)(2,1)}, u32[]{:S(2)}) copy-start(bf16[2048,112]{0,1:T(8,128)(2,1)} %param.19) | copy-start | bytes 1376260
  1.9 28.7 %all-to-all-start = ((bf16[64,3,2,128]{3,2,1,0:T(2,128)(2,1)}), bf16[64,3,2,128]{3,2,1,0:T(2,128)(2,1)S(1)}, u32[]{:S(2)}, u32[]{:S(2)}) async-start(bf16[64,3,2,128]{3,2,1,0:T(2,128)(2,1)} %shard_map.100), calls=%async_computation | async-start | bytes 196608 | tf_op jit(solution)/shard_map/all_to_all | solution.py:183
  25.0 1.0 %copy-start.1 = (bf16[1,512,512]{2,1,0:T(8,128)(2,1)S(1)}, bf16[1,512,512]{2,1,0:T(8,128)(2,1)}, u32[]{:S(2)}) copy-start(bf16[1,512,512]{2,1,0:T(8,128)(2,1)} %param.12) | copy-start | bytes 1572868
  26.8 4.4 %collective-permute-start = (bf16[112,1024]{1,0:T(8,128)(2,1)S(1)}, bf16[112,1024]{1,0:T(8,128)(2,1)S(1)}, u32[]{:S(2)}, u32[]{:S(2)}) collective-permute-start(bf16[112,1024]{1,0:T(8,128)(2,1)S(1)} %constant_dynamic-slice_fusion), channel_id=1, source_target_pairs={{0,1},{1,0},{2,3},{3,2},{4,5},{5,4},{6,7},{7,6},{8,9},{9,8},{10,11... | collective-permute-start | bytes 688136 | tf_op jit(solution)/shard_map/ppermute | solution.py:228
